TPU v7x, 32 devices: a whole 2x2x4 slice. The times are simulated.
32 devices in a mesh: gx: 4 (over y, core), gy: 2 (over x), gz: 4 (over z).
Axes of the slice: x: 2, y: 2, z: 4, core: 2. Of those that a mesh axis runs over, the one named last changes fastest.
Arguments:
- source_field: float32 [2, 64, 32, 512], P(None, 'gx', 'gy', 'gz'), may hold values from -6 to 6
- mach_number: bfloat16 [64, 32, 512], P('gx', 'gy', 'gz'), may hold values from 0.14941406 to 0.59765625
Outputs:
- correction: float32 [2, 64, 32, 512], P(None, 'gx', 'gy', 'gz')
All inputs are finite; a program needn't handle non-finite values.
Results may differ from a plain program's by a relative error of at most 0.0003.
Values sent between devices are 32-bit elements; how exact they have to be, the bound alone decides.
A program may use at most 128 MiB of HBM per device.

v0:
```python
import jax
import jax.numpy as jnp
from jax import lax
from jax.sharding import PartitionSpec as P

LEVELS = 5
POST = 2
COARSE_SWEEPS = 6


wave_step = 0.25
jacobi_weight = 0.5


def extended(block, sides, width):
    for axis, dim in sides:
        count = lax.axis_size(axis)
        forward = [(i, i + 1) for i in range(count - 1)]
        backward = [(target, source) for source, target in forward]
        low = lax.ppermute(
            lax.slice_in_dim(block, block.shape[dim] - width, None, axis=dim), axis, forward
        )
        high = lax.ppermute(lax.slice_in_dim(block, 0, width, axis=dim), axis, backward)
        block = jnp.concatenate([low, block, high], axis=dim)
    return block


def complex_times(values, factor):
    real_part = values[0] * factor[0] - values[1] * factor[1]
    imaginary = values[0] * factor[1] + values[1] * factor[0]
    return jnp.stack([real_part, imaginary])


def inverse_diagonal(mach_field, grid_level):
    diffusion_scale = 0.25**grid_level
    wave_square = wave_step * wave_step
    axial_weight = 1.0 - mach_field * mach_field
    diagonal_real = diffusion_scale * (2.0 * axial_weight + 4.0) - wave_square
    diagonal_imaginary = 0.5 * wave_square
    modulus = diagonal_real * diagonal_real + diagonal_imaginary * diagonal_imaginary
    return jnp.stack([diagonal_real / modulus, -diagonal_imaginary / modulus])


def operate(padded, mach_field, grid_level):
    centre = padded[:, 1:-1, 1:-1, 1:-1]
    east_cells = padded[:, 2:, 1:-1, 1:-1]
    west_cells = padded[:, :-2, 1:-1, 1:-1]
    north_cells = padded[:, 1:-1, 2:, 1:-1]
    south_cells = padded[:, 1:-1, :-2, 1:-1]
    upper_cells = padded[:, 1:-1, 1:-1, 2:]
    lower_cells = padded[:, 1:-1, 1:-1, :-2]
    diffusion_scale = 0.25**grid_level
    axial_weight = 1.0 - mach_field * mach_field
    spread = diffusion_scale * (
        axial_weight * (2.0 * centre - east_cells - west_cells)
        + (2.0 * centre - north_cells - south_cells)
        + (2.0 * centre - upper_cells - lower_cells)
    )
    advect = wave_step * 0.5**grid_level * mach_field
    axial_slope = east_cells - west_cells
    wave_square = wave_step * wave_step
    real_part = spread[0] + advect * axial_slope[1] - wave_square * (centre[0] + 0.5 * centre[1])
    imaginary = spread[1] - advect * axial_slope[0] - wave_square * (centre[1] - 0.5 * centre[0])
    return jnp.stack([real_part, imaginary])


def jacobi_step(solution, padded, source, mach_field, inverse, grid_level):
    return solution + jacobi_weight * complex_times(
        source - operate(padded, mach_field, grid_level), inverse
    )


def restrict(values):
    leading = values.shape[:-3]
    leading_rank = len(leading)
    first_length, second_length, third_length = values.shape[-3:]
    grouped = values.reshape(
        leading + (first_length // 2, 2, second_length // 2, 2, third_length // 2, 2)
    )
    return grouped.mean(axis=(leading_rank + 1, leading_rank + 3, leading_rank + 5))


def prolong(values):
    leading = values.shape[:-3]
    first_length, second_length, third_length = values.shape[-3:]
    expanded = values[..., :, None, :, None, :, None]
    expanded = jnp.broadcast_to(
        expanded, leading + (first_length, 2, second_length, 2, third_length, 2)
    )
    return expanded.reshape(leading + (2 * first_length, 2 * second_length, 2 * third_length))


def sweep_halo(solution):
    return extended(solution, (("gx", 1), ("gy", 2), ("gz", 3)), 1)


def coarse_solve(source, mach_field, grid_level):
    inverse = inverse_diagonal(mach_field, grid_level)
    solution = jacobi_weight * complex_times(source, inverse)
    for sweep_index in range(COARSE_SWEEPS - 1):
        padded = extended(solution, (("gx", 1), ("gy", 2), ("gz", 3)), 1)
        solution = jacobi_step(solution, padded, source, mach_field, inverse, grid_level)
    return solution


def multigrid(source, mach_levels, grid_level):
    mach_field = mach_levels[grid_level]
    if grid_level == LEVELS - 1:
        return coarse_solve(source, mach_field, grid_level)
    inverse = inverse_diagonal(mach_field, grid_level)
    solution = jacobi_weight * complex_times(source, inverse)
    solution = jacobi_step(solution, sweep_halo(solution), source, mach_field, inverse, grid_level)
    padded = extended(solution, (("gx", 1), ("gy", 2), ("gz", 3)), 1)
    residual = source - operate(padded, mach_field, grid_level)
    coarse = multigrid(restrict(residual), mach_levels, grid_level + 1)
    solution = solution + prolong(coarse)
    for sweep_index in range(POST):
        solution = jacobi_step(
            solution, sweep_halo(solution), source, mach_field, inverse, grid_level
        )
    return solution


def shards(source_field, mach_number):
    mach_levels = [mach_number.astype(jnp.float32)]
    for grid_level in range(1, LEVELS):
        mach_levels.append(restrict(mach_levels[-1]))
    return multigrid(source_field, mach_levels, 0)


def solution(mesh):
    return jax.shard_map(
        shards,
        mesh=mesh,
        in_specs=(P(None, "gx", "gy", "gz"), P("gx", "gy", "gz")),
        out_specs=P(None, "gx", "gy", "gz"),
        check_vma=False,
    )
```

profile of v0, /device:TPU:0, one launch (start us, length us, event | category | flops | bytes accessed | tf_op | source)
XLA Modules:
  0.0 564.4 jit_solution(2950116160305532142)
XLA Ops:
  7.6 4.8 collective-permute-start.3
  15.6 5.3 collective-permute-start.5
  20.9 8.5 %collective-permute-done.4 = f32[2,18,18,1]{3,2,1,0:T(8,128)S(1)} collective-permute-done((f32[2,18,18,1]{3,2,1,0:T(8,128)S(1)}, f32[2,18,18,1]{3,2,1,0:T(8,128)S(1)}, u32[]{:S(2)}, u32[]{:S(2)}) %collective-permute-start.4) | collective-permute-done | bytes 2624 | tf_op jit(solution)/shard_map/ppermute | solution.py:23
  37.8 4.6 collective-permute-start.9
  42.4 9.7 %reshape.1671 = f32[8,2,8,2,64,2]{5,4,3,2,1,0:T(8,128)} reshape(bf16[16,16,128]{2,1,0:T(8,128)(2,1)S(1)} %copy-done.1) | data formatting | bytes 196608 | tf_op jit(solution)/shard_map/reshape | solution.py:77
  57.7 5.0 collective-permute-start.11
  62.7 8.4 %collective-permute-done.10 = f32[2,18,18,1]{3,2,1,0:T(8,128)S(1)} collective-permute-done((f32[2,18,18,1]{3,2,1,0:T(8,128)S(1)}, f32[2,18,18,1]{3,2,1,0:T(8,128)S(1)}, u32[]{:S(2)}, u32[]{:S(2)}) %collective-permute-start.10) | collective-permute-done | bytes 2624 | tf_op jit(solution)/shard_map/ppermute | solution.py:23
  72.8 18.1 %reshape.1670 = f32[2,8,2,8,2,64,2]{6,5,4,3,2,1,0:T(8,128)} reshape(f32[2,16,16,128]{3,2,1,0:T(8,128)S(1)} %maximum_subtract_fusion.2) | data formatting | bytes 524288 | tf_op jit(solution)/shard_map/reshape | solution.py:77
  90.9 7.0 %reduce_sum.86 = f32[2,8,8,64]{3,2,1,0:T(8,128)S(1)} reduce(f32[2,8,2,8,2,64,2]{6,5,4,3,2,1,0:T(8,128)} %reshape.1670, f32[]{:T(128)} %constant.31.clone.1), dimensions={2,4,6}, to_apply=%region_0.0 | reduce | flops 57344 | bytes 294916 | tf_op jit(solution)/shard_map/reduce_sum | solution.py:80
  104.5 4.5 collective-permute-start.15
  111.8 5.0 collective-permute-start.17
  126.5 4.5 collective-permute-start.21
  136.0 5.2 collective-permute-start.23
  158.9 4.5 collective-permute-start.27
  166.1 4.9 collective-permute-start.29
  179.5 4.5 collective-permute-start.33
  186.8 5.0 collective-permute-start.35
  195.4 4.6 collective-permute-start.37
  202.2 4.5 collective-permute-start.39
  209.4 4.6 collective-permute-start.41
  216.9 5.0 collective-permute-start.43
  224.1 4.5 collective-permute-start.45
  231.3 4.5 collective-permute-start.47
  238.9 5.0 collective-permute-start.49
  246.0 4.5 collective-permute-start.51
  253.3 4.5 collective-permute-start.53
  260.7 5.0 collective-permute-start.55
  267.8 4.5 collective-permute-start.57
  275.0 4.5 collective-permute-start.59
  282.4 5.0 collective-permute-start.61
  289.5 4.5 collective-permute-start.63
  296.7 4.5 collective-permute-start.65
  304.1 5.0 collective-permute-start.67
  311.2 4.5 collective-permute-start.69
  318.4 4.5 collective-permute-start.71
  325.8 5.0 collective-permute-start.73
  332.9 4.5 collective-permute-start.75
  340.2 4.5 collective-permute-start.77
  347.7 5.0 collective-permute-start.79
  354.9 4.5 collective-permute-start.81
  362.1 4.5 collective-permute-start.83
  369.6 5.0 collective-permute-start.85
  376.7 4.5 collective-permute-start.87
  384.0 4.5 collective-permute-start.89
  391.7 5.0 collective-permute-start.91
  406.1 4.5 collective-permute-start.95
  413.9 5.0 collective-permute-start.97
  428.4 4.6 collective-permute-start.101
  438.3 5.0 collective-permute-start.103
  445.5 4.5 collective-permute-start.105
  452.9 4.6 collective-permute-start.107
  461.9 5.1 collective-permute-start.109
  469.1 4.5 collective-permute-start.111
  476.4 4.7 collective-permute-start.113
  484.3 6.5 %broadcast_in_dim.17 = f32[2,8,2,8,2,64,2]{6,5,4,3,2,1,0:T(8,128)} broadcast(f32[2,8,8,64]{3,2,1,0:T(8,128)S(1)} %fusion.115), dimensions={0,1,3,5} | broadcast | bytes 294912 | tf_op jit(solution)/shard_map/broadcast_in_dim | solution.py:87
  490.7 12.7 %reshape.1674 = f32[2,16,16,128]{3,2,1,0:T(8,128)S(1)} reshape(f32[2,8,2,8,2,64,2]{6,5,4,3,2,1,0:T(8,128)} %broadcast_in_dim.17) | data formatting | bytes 524288 | tf_op jit(solution)/shard_map/reshape | solution.py:90
  504.8 5.1 collective-permute-start.115
  512.1 4.5 collective-permute-start.117
  519.6 4.7 collective-permute-start.119
  524.4 6.2 %collective-permute-done.118 = f32[2,18,18,1]{3,2,1,0:T(8,128)S(1)} collective-permute-done((f32[2,18,18,1]{3,2,1,0:T(8,128)S(1)}, f32[2,18,18,1]{3,2,1,0:T(8,128)S(1)}, u32[]{:S(2)}, u32[]{:S(2)}) %collective-permute-start.118) | collective-permute-done | bytes 2624 | tf_op jit(solution)/shard_map/ppermute | solution.py:23
  534.3 5.2 collective-permute-start.121
  541.7 4.5 collective-permute-start.123
  549.2 4.7 collective-permute-start.125
  554.0 7.3 %collective-permute-done.124 = f32[2,18,18,1]{3,2,1,0:T(8,128)S(1)} collective-permute-done((f32[2,18,18,1]{3,2,1,0:T(8,128)S(1)}, f32[2,18,18,1]{3,2,1,0:T(8,128)S(1)}, u32[]{:S(2)}, u32[]{:S(2)}) %collective-permute-start.124) | collective-permute-done | bytes 2624 | tf_op jit(solution)/shard_map/ppermute | solution.py:23
  (480 shorter events, 216.3 us)
Async XLA Ops:
  6.3 6.2 %collective-permute-start.2 = (f32[2,18,1,128]{3,2,1,0:T(1,128)S(1)}, f32[2,18,1,128]{3,2,1,0:T(1,128)S(1)}, u32[]{:S(2)}, u32[]{:S(2)}) collective-permute-start(f32[2,18,1,128]{3,2,1,0:T(1,128)S(1)} %get-tuple-element.36), channel_id=1, source_target_pairs={{4,0},{5,1},{6,2},{7,3},{12,8},{13,9},{14,10},{15,11},{20,16},{21,... | collective-permute-start | bytes 55304 | tf_op jit(solution)/shard_map/ppermute | solution.py:23
  7.6 6.3 %collective-permute-start.3 = (f32[2,18,1,128]{3,2,1,0:T(1,128)S(1)}, f32[2,18,1,128]{3,2,1,0:T(1,128)S(1)}, u32[]{:S(2)}, u32[]{:S(2)}) collective-permute-start(f32[2,18,1,128]{3,2,1,0:T(1,128)S(1)} %get-tuple-element.35), channel_id=1, source_target_pairs={{0,4},{1,5},{2,6},{3,7},{8,12},{9,13},{10,14},{11,15},{16,20},{17,... | collective-permute-start | bytes 55304 | tf_op jit(solution)/shard_map/ppermute | solution.py:20
  14.2 15.3 %collective-permute-start.4 = (f32[2,18,18,1]{3,2,1,0:T(8,128)S(1)}, f32[2,18,18,1]{3,2,1,0:T(8,128)S(1)}, u32[]{:S(2)}, u32[]{:S(2)}) collective-permute-start(f32[2,18,18,1]{3,2,1,0:T(8,128)S(1)} %get-tuple-element.19), channel_id=1, source_target_pairs={{1,0},{2,1},{3,2},{5,4},{6,5},{7,6},{9,8},{10,9},{11,10},{13,12},{... | collective-permute-start | bytes 7784 | tf_op jit(solution)/shard_map/ppermute | solution.py:23
  15.6 15.0 %collective-permute-start.5 = (f32[2,18,18,1]{3,2,1,0:T(8,128)S(1)}, f32[2,18,18,1]{3,2,1,0:T(8,128)S(1)}, u32[]{:S(2)}, u32[]{:S(2)}) collective-permute-start(f32[2,18,18,1]{3,2,1,0:T(8,128)S(1)} %get-tuple-element.20), channel_id=1, source_target_pairs={{0,1},{1,2},{2,3},{4,5},{5,6},{6,7},{8,9},{9,10},{10,11},{12,13},{... | collective-permute-start | bytes 7784 | tf_op jit(solution)/shard_map/ppermute | solution.py:20
  36.5 19.5 %collective-permute-start.8 = (f32[2,18,1,128]{3,2,1,0:T(1,128)S(1)}, f32[2,18,1,128]{3,2,1,0:T(1,128)S(1)}, u32[]{:S(2)}, u32[]{:S(2)}) collective-permute-start(f32[2,18,1,128]{3,2,1,0:T(1,128)S(1)} %get-tuple-element.34), channel_id=1, source_target_pairs={{4,0},{5,1},{6,2},{7,3},{12,8},{13,9},{14,10},{15,11},{20,16},{21,... | collective-permute-start | bytes 55304 | tf_op jit(solution)/shard_map/ppermute | solution.py:23
  37.8 18.3 %collective-permute-start.9 = (f32[2,18,1,128]{3,2,1,0:T(1,128)S(1)}, f32[2,18,1,128]{3,2,1,0:T(1,128)S(1)}, u32[]{:S(2)}, u32[]{:S(2)}) collective-permute-start(f32[2,18,1,128]{3,2,1,0:T(1,128)S(1)} %get-tuple-element.33), channel_id=1, source_target_pairs={{0,4},{1,5},{2,6},{3,7},{8,12},{9,13},{10,14},{11,15},{16,20},{17,... | collective-permute-start | bytes 55304 | tf_op jit(solution)/shard_map/ppermute | solution.py:20
  56.4 14.8 %collective-permute-start.10 = (f32[2,18,18,1]{3,2,1,0:T(8,128)S(1)}, f32[2,18,18,1]{3,2,1,0:T(8,128)S(1)}, u32[]{:S(2)}, u32[]{:S(2)}) collective-permute-start(f32[2,18,18,1]{3,2,1,0:T(8,128)S(1)} %get-tuple-element.17), channel_id=1, source_target_pairs={{1,0},{2,1},{3,2},{5,4},{6,5},{7,6},{9,8},{10,9},{11,10},{13,12},{... | collective-permute-start | bytes 7784 | tf_op jit(solution)/shard_map/ppermute | solution.py:23
  57.7 14.7 %collective-permute-start.11 = (f32[2,18,18,1]{3,2,1,0:T(8,128)S(1)}, f32[2,18,18,1]{3,2,1,0:T(8,128)S(1)}, u32[]{:S(2)}, u32[]{:S(2)}) collective-permute-start(f32[2,18,18,1]{3,2,1,0:T(8,128)S(1)} %get-tuple-element.18), channel_id=1, source_target_pairs={{0,1},{1,2},{2,3},{4,5},{5,6},{6,7},{8,9},{9,10},{10,11},{12,13},{... | collective-permute-start | bytes 7784 | tf_op jit(solution)/shard_map/ppermute | solution.py:20
  104.5 5.9 %collective-permute-start.15 = (f32[2,10,1,64]{3,2,1,0:T(1,128)S(1)}, f32[2,10,1,64]{3,2,1,0:T(1,128)S(1)}, u32[]{:S(2)}, u32[]{:S(2)}) collective-permute-start(f32[2,10,1,64]{3,2,1,0:T(1,128)S(1)} %get-tuple-element.75), channel_id=1, source_target_pairs={{0,4},{1,5},{2,6},{3,7},{8,12},{9,13},{10,14},{11,15},{16,20},{17,... | collective-permute-start | bytes 15368 | tf_op jit(solution)/shard_map/ppermute | solution.py:20
  110.5 8.0 %collective-permute-start.16 = (f32[2,10,10,1]{3,2,1,0:T(8,128)S(1)}, f32[2,10,10,1]{3,2,1,0:T(8,128)S(1)}, u32[]{:S(2)}, u32[]{:S(2)}) collective-permute-start(f32[2,10,10,1]{3,2,1,0:T(8,128)S(1)} %get-tuple-element.59), channel_id=1, source_target_pairs={{1,0},{2,1},{3,2},{5,4},{6,5},{7,6},{9,8},{10,9},{11,10},{13,12},{... | collective-permute-start | bytes 2408 | tf_op jit(solution)/shard_map/ppermute | solution.py:23
  111.8 7.9 %collective-permute-start.17 = (f32[2,10,10,1]{3,2,1,0:T(8,128)S(1)}, f32[2,10,10,1]{3,2,1,0:T(8,128)S(1)}, u32[]{:S(2)}, u32[]{:S(2)}) collective-permute-start(f32[2,10,10,1]{3,2,1,0:T(8,128)S(1)} %get-tuple-element.60), channel_id=1, source_target_pairs={{0,1},{1,2},{2,3},{4,5},{5,6},{6,7},{8,9},{9,10},{10,11},{12,13},{... | collective-permute-start | bytes 2408 | tf_op jit(solution)/shard_map/ppermute | solution.py:20
  125.2 9.3 %collective-permute-start.20 = (f32[2,10,1,64]{3,2,1,0:T(1,128)S(1)}, f32[2,10,1,64]{3,2,1,0:T(1,128)S(1)}, u32[]{:S(2)}, u32[]{:S(2)}) collective-permute-start(f32[2,10,1,64]{3,2,1,0:T(1,128)S(1)} %get-tuple-element.74), channel_id=1, source_target_pairs={{4,0},{5,1},{6,2},{7,3},{12,8},{13,9},{14,10},{15,11},{20,16},{21,... | collective-permute-start | bytes 15368 | tf_op jit(solution)/shard_map/ppermute | solution.py:23
  126.5 8.0 %collective-permute-start.21 = (f32[2,10,1,64]{3,2,1,0:T(1,128)S(1)}, f32[2,10,1,64]{3,2,1,0:T(1,128)S(1)}, u32[]{:S(2)}, u32[]{:S(2)}) collective-permute-start(f32[2,10,1,64]{3,2,1,0:T(1,128)S(1)} %get-tuple-element.73), channel_id=1, source_target_pairs={{0,4},{1,5},{2,6},{3,7},{8,12},{9,13},{10,14},{11,15},{16,20},{17,... | collective-permute-start | bytes 15368 | tf_op jit(solution)/shard_map/ppermute | solution.py:20
  134.7 8.6 %collective-permute-start.22 = (f32[2,10,10,1]{3,2,1,0:T(8,128)S(1)}, f32[2,10,10,1]{3,2,1,0:T(8,128)S(1)}, u32[]{:S(2)}, u32[]{:S(2)}) collective-permute-start(f32[2,10,10,1]{3,2,1,0:T(8,128)S(1)} %get-tuple-element.57), channel_id=1, source_target_pairs={{1,0},{2,1},{3,2},{5,4},{6,5},{7,6},{9,8},{10,9},{11,10},{13,12},{... | collective-permute-start | bytes 2408 | tf_op jit(solution)/shard_map/ppermute | solution.py:23
  136.0 9.1 %collective-permute-start.23 = (f32[2,10,10,1]{3,2,1,0:T(8,128)S(1)}, f32[2,10,10,1]{3,2,1,0:T(8,128)S(1)}, u32[]{:S(2)}, u32[]{:S(2)}) collective-permute-start(f32[2,10,10,1]{3,2,1,0:T(8,128)S(1)} %get-tuple-element.58), channel_id=1, source_target_pairs={{0,1},{1,2},{2,3},{4,5},{5,6},{6,7},{8,9},{9,10},{10,11},{12,13},{... | collective-permute-start | bytes 2408 | tf_op jit(solution)/shard_map/ppermute | solution.py:20
  164.8 6.3 %collective-permute-start.28 = (f32[2,6,6,1]{3,2,1,0:T(8,128)S(1)}, f32[2,6,6,1]{3,2,1,0:T(8,128)S(1)}, u32[]{:S(2)}, u32[]{:S(2)}) collective-permute-start(f32[2,6,6,1]{3,2,1,0:T(8,128)S(1)} %get-tuple-element.100), channel_id=1, source_target_pairs={{1,0},{2,1},{3,2},{5,4},{6,5},{7,6},{9,8},{10,9},{11,10},{13,12},{... | collective-permute-start | bytes 872 | tf_op jit(solution)/shard_map/ppermute | solution.py:23
  166.1 6.7 %collective-permute-start.29 = (f32[2,6,6,1]{3,2,1,0:T(8,128)S(1)}, f32[2,6,6,1]{3,2,1,0:T(8,128)S(1)}, u32[]{:S(2)}, u32[]{:S(2)}) collective-permute-start(f32[2,6,6,1]{3,2,1,0:T(8,128)S(1)} %get-tuple-element.101), channel_id=1, source_target_pairs={{0,1},{1,2},{2,3},{4,5},{5,6},{6,7},{8,9},{9,10},{10,11},{12,13},{... | collective-permute-start | bytes 872 | tf_op jit(solution)/shard_map/ppermute | solution.py:20
  178.2 6.2 %collective-permute-start.32 = (f32[2,6,1,32]{3,2,1,0:T(1,128)S(1)}, f32[2,6,1,32]{3,2,1,0:T(1,128)S(1)}, u32[]{:S(2)}, u32[]{:S(2)}) collective-permute-start(f32[2,6,1,32]{3,2,1,0:T(1,128)S(1)} %get-tuple-element.113), channel_id=1, source_target_pairs={{4,0},{5,1},{6,2},{7,3},{12,8},{13,9},{14,10},{15,11},{20,16},{21,... | collective-permute-start | bytes 4616 | tf_op jit(solution)/shard_map/ppermute | solution.py:23
  185.5 6.4 %collective-permute-start.34 = (f32[2,6,6,1]{3,2,1,0:T(8,128)S(1)}, f32[2,6,6,1]{3,2,1,0:T(8,128)S(1)}, u32[]{:S(2)}, u32[]{:S(2)}) collective-permute-start(f32[2,6,6,1]{3,2,1,0:T(8,128)S(1)} %get-tuple-element.98), channel_id=1, source_target_pairs={{1,0},{2,1},{3,2},{5,4},{6,5},{7,6},{9,8},{10,9},{11,10},{13,12},{... | collective-permute-start | bytes 872 | tf_op jit(solution)/shard_map/ppermute | solution.py:23
  186.8 6.7 %collective-permute-start.35 = (f32[2,6,6,1]{3,2,1,0:T(8,128)S(1)}, f32[2,6,6,1]{3,2,1,0:T(8,128)S(1)}, u32[]{:S(2)}, u32[]{:S(2)}) collective-permute-start(f32[2,6,6,1]{3,2,1,0:T(8,128)S(1)} %get-tuple-element.99), channel_id=1, source_target_pairs={{0,1},{1,2},{2,3},{4,5},{5,6},{6,7},{8,9},{9,10},{10,11},{12,13},{... | collective-permute-start | bytes 872 | tf_op jit(solution)/shard_map/ppermute | solution.py:20
  194.1 5.9 %collective-permute-start.36 = (f32[2,1,2,16]{3,2,1,0:T(2,128)S(1)}, f32[2,1,2,16]{3,2,1,0:T(2,128)S(1)}, u32[]{:S(2)}, u32[]{:S(2)}) collective-permute-start(f32[2,1,2,16]{3,2,1,0:T(2,128)S(1)} %get-tuple-element.179), channel_id=1, source_target_pairs={{8,0},{16,8},{24,16},{9,1},{17,9},{25,17},{10,2},{18,10},{26,18},{... | collective-permute-start | bytes 776 | tf_op jit(solution)/shard_map/ppermute | solution.py:23
  208.1 5.9 %collective-permute-start.40 = (f32[2,4,4,1]{3,2,1,0:T(4,128)S(1)}, f32[2,4,4,1]{3,2,1,0:T(4,128)S(1)}, u32[]{:S(2)}, u32[]{:S(2)}) collective-permute-start(f32[2,4,4,1]{3,2,1,0:T(4,128)S(1)} %get-tuple-element.130), channel_id=1, source_target_pairs={{1,0},{2,1},{3,2},{5,4},{6,5},{7,6},{9,8},{10,9},{11,10},{13,12},{... | collective-permute-start | bytes 392 | tf_op jit(solution)/shard_map/ppermute | solution.py:23
  209.4 6.0 %collective-permute-start.41 = (f32[2,4,4,1]{3,2,1,0:T(4,128)S(1)}, f32[2,4,4,1]{3,2,1,0:T(4,128)S(1)}, u32[]{:S(2)}, u32[]{:S(2)}) collective-permute-start(f32[2,4,4,1]{3,2,1,0:T(4,128)S(1)} %get-tuple-element.131), channel_id=1, source_target_pairs={{0,1},{1,2},{2,3},{4,5},{5,6},{6,7},{8,9},{9,10},{10,11},{12,13},{... | collective-permute-start | bytes 392 | tf_op jit(solution)/shard_map/ppermute | solution.py:20
  215.6 6.3 %collective-permute-start.42 = (f32[2,1,2,16]{3,2,1,0:T(2,128)S(1)}, f32[2,1,2,16]{3,2,1,0:T(2,128)S(1)}, u32[]{:S(2)}, u32[]{:S(2)}) collective-permute-start(f32[2,1,2,16]{3,2,1,0:T(2,128)S(1)} %get-tuple-element.177), channel_id=1, source_target_pairs={{8,0},{16,8},{24,16},{9,1},{17,9},{25,17},{10,2},{18,10},{26,18},{... | collective-permute-start | bytes 776 | tf_op jit(solution)/shard_map/ppermute | solution.py:23
  222.8 6.1 %collective-permute-start.44 = (f32[2,4,1,16]{3,2,1,0:T(1,128)S(1)}, f32[2,4,1,16]{3,2,1,0:T(1,128)S(1)}, u32[]{:S(2)}, u32[]{:S(2)}) collective-permute-start(f32[2,4,1,16]{3,2,1,0:T(1,128)S(1)} %get-tuple-element.159), channel_id=1, source_target_pairs={{4,0},{5,1},{6,2},{7,3},{12,8},{13,9},{14,10},{15,11},{20,16},{21,... | collective-permute-start | bytes 1544 | tf_op jit(solution)/shard_map/ppermute | solution.py:23
  231.3 6.0 %collective-permute-start.47 = (f32[2,4,4,1]{3,2,1,0:T(4,128)S(1)}, f32[2,4,4,1]{3,2,1,0:T(4,128)S(1)}, u32[]{:S(2)}, u32[]{:S(2)}) collective-permute-start(f32[2,4,4,1]{3,2,1,0:T(4,128)S(1)} %get-tuple-element.129), channel_id=1, source_target_pairs={{0,1},{1,2},{2,3},{4,5},{5,6},{6,7},{8,9},{9,10},{10,11},{12,13},{... | collective-permute-start | bytes 392 | tf_op jit(solution)/shard_map/ppermute | solution.py:20
  237.6 6.3 %collective-permute-start.48 = (f32[2,1,1,8]{3,2,1,0:T(1,128)S(1)}, f32[2,1,1,8]{3,2,1,0:T(1,128)S(1)}, u32[]{:S(2)}, u32[]{:S(2)}) collective-permute-start(f32[2,1,1,8]{3,2,1,0:T(1,128)S(1)} %broadcast_multiply_fusion.9), channel_id=1, source_target_pairs={{8,0},{16,8},{24,16},{9,1},{17,9},{25,17},{10,2},{18,10},{26,18},{... | collective-permute-start | bytes 200 | tf_op jit(solution)/shard_map/ppermute | solution.py:23
  253.3 5.9 %collective-permute-start.53 = (f32[2,3,3,1]{3,2,1,0:T(4,128)S(1)}, f32[2,3,3,1]{3,2,1,0:T(4,128)S(1)}, u32[]{:S(2)}, u32[]{:S(2)}) collective-permute-start(f32[2,3,3,1]{3,2,1,0:T(4,128)S(1)} %get-tuple-element.153), channel_id=1, source_target_pairs={{0,1},{1,2},{2,3},{4,5},{5,6},{6,7},{8,9},{9,10},{10,11},{12,13},{... | collective-permute-start | bytes 224 | tf_op jit(solution)/shard_map/ppermute | solution.py:20
  259.4 6.3 %collective-permute-start.54 = (f32[2,1,1,8]{3,2,1,0:T(1,128)S(1)}, f32[2,1,1,8]{3,2,1,0:T(1,128)S(1)}, u32[]{:S(2)}, u32[]{:S(2)}) collective-permute-start(f32[2,1,1,8]{3,2,1,0:T(1,128)S(1)} %fusion.280), channel_id=1, source_target_pairs={{8,0},{16,8},{24,16},{9,1},{17,9},{25,17},{10,2},{18,10},{26,18},{... | collective-permute-start | bytes 200 | tf_op jit(solution)/shard_map/ppermute | solution.py:23
  275.0 5.9 %collective-permute-start.59 = (f32[2,3,3,1]{3,2,1,0:T(4,128)S(1)}, f32[2,3,3,1]{3,2,1,0:T(4,128)S(1)}, u32[]{:S(2)}, u32[]{:S(2)}) collective-permute-start(f32[2,3,3,1]{3,2,1,0:T(4,128)S(1)} %get-tuple-element.151), channel_id=1, source_target_pairs={{0,1},{1,2},{2,3},{4,5},{5,6},{6,7},{8,9},{9,10},{10,11},{12,13},{... | collective-permute-start | bytes 224 | tf_op jit(solution)/shard_map/ppermute | solution.py:20
  281.1 6.3 %collective-permute-start.60 = (f32[2,1,1,8]{3,2,1,0:T(1,128)S(1)}, f32[2,1,1,8]{3,2,1,0:T(1,128)S(1)}, u32[]{:S(2)}, u32[]{:S(2)}) collective-permute-start(f32[2,1,1,8]{3,2,1,0:T(1,128)S(1)} %fusion.281), channel_id=1, source_target_pairs={{8,0},{16,8},{24,16},{9,1},{17,9},{25,17},{10,2},{18,10},{26,18},{... | collective-permute-start | bytes 200 | tf_op jit(solution)/shard_map/ppermute | solution.py:23
  296.7 5.9 %collective-permute-start.65 = (f32[2,3,3,1]{3,2,1,0:T(4,128)S(1)}, f32[2,3,3,1]{3,2,1,0:T(4,128)S(1)}, u32[]{:S(2)}, u32[]{:S(2)}) collective-permute-start(f32[2,3,3,1]{3,2,1,0:T(4,128)S(1)} %get-tuple-element.149), channel_id=1, source_target_pairs={{0,1},{1,2},{2,3},{4,5},{5,6},{6,7},{8,9},{9,10},{10,11},{12,13},{... | collective-permute-start | bytes 224 | tf_op jit(solution)/shard_map/ppermute | solution.py:20
  302.8 6.3 %collective-permute-start.66 = (f32[2,1,1,8]{3,2,1,0:T(1,128)S(1)}, f32[2,1,1,8]{3,2,1,0:T(1,128)S(1)}, u32[]{:S(2)}, u32[]{:S(2)}) collective-permute-start(f32[2,1,1,8]{3,2,1,0:T(1,128)S(1)} %fusion.282), channel_id=1, source_target_pairs={{8,0},{16,8},{24,16},{9,1},{17,9},{25,17},{10,2},{18,10},{26,18},{... | collective-permute-start | bytes 200 | tf_op jit(solution)/shard_map/ppermute | solution.py:23
  318.4 5.9 %collective-permute-start.71 = (f32[2,3,3,1]{3,2,1,0:T(4,128)S(1)}, f32[2,3,3,1]{3,2,1,0:T(4,128)S(1)}, u32[]{:S(2)}, u32[]{:S(2)}) collective-permute-start(f32[2,3,3,1]{3,2,1,0:T(4,128)S(1)} %get-tuple-element.147), channel_id=1, source_target_pairs={{0,1},{1,2},{2,3},{4,5},{5,6},{6,7},{8,9},{9,10},{10,11},{12,13},{... | collective-permute-start | bytes 224 | tf_op jit(solution)/shard_map/ppermute | solution.py:20
  324.5 6.3 %collective-permute-start.72 = (f32[2,1,1,8]{3,2,1,0:T(1,128)S(1)}, f32[2,1,1,8]{3,2,1,0:T(1,128)S(1)}, u32[]{:S(2)}, u32[]{:S(2)}) collective-permute-start(f32[2,1,1,8]{3,2,1,0:T(1,128)S(1)} %fusion.283), channel_id=1, source_target_pairs={{8,0},{16,8},{24,16},{9,1},{17,9},{25,17},{10,2},{18,10},{26,18},{... | collective-permute-start | bytes 200 | tf_op jit(solution)/shard_map/ppermute | solution.py:23
  340.2 5.9 %collective-permute-start.77 = (f32[2,3,3,1]{3,2,1,0:T(4,128)S(1)}, f32[2,3,3,1]{3,2,1,0:T(4,128)S(1)}, u32[]{:S(2)}, u32[]{:S(2)}) collective-permute-start(f32[2,3,3,1]{3,2,1,0:T(4,128)S(1)} %get-tuple-element.145), channel_id=1, source_target_pairs={{0,1},{1,2},{2,3},{4,5},{5,6},{6,7},{8,9},{9,10},{10,11},{12,13},{... | collective-permute-start | bytes 224 | tf_op jit(solution)/shard_map/ppermute | solution.py:20
  346.4 6.3 %collective-permute-start.78 = (f32[2,1,2,16]{3,2,1,0:T(2,128)S(1)}, f32[2,1,2,16]{3,2,1,0:T(2,128)S(1)}, u32[]{:S(2)}, u32[]{:S(2)}) collective-permute-start(f32[2,1,2,16]{3,2,1,0:T(2,128)S(1)} %get-tuple-element.175), channel_id=1, source_target_pairs={{8,0},{16,8},{24,16},{9,1},{17,9},{25,17},{10,2},{18,10},{26,18},{... | collective-permute-start | bytes 776 | tf_op jit(solution)/shard_map/ppermute | solution.py:23
  362.1 6.0 %collective-permute-start.83 = (f32[2,4,4,1]{3,2,1,0:T(4,128)S(1)}, f32[2,4,4,1]{3,2,1,0:T(4,128)S(1)}, u32[]{:S(2)}, u32[]{:S(2)}) collective-permute-start(f32[2,4,4,1]{3,2,1,0:T(4,128)S(1)} %get-tuple-element.127), channel_id=1, source_target_pairs={{0,1},{1,2},{2,3},{4,5},{5,6},{6,7},{8,9},{9,10},{10,11},{12,13},{... | collective-permute-start | bytes 392 | tf_op jit(solution)/shard_map/ppermute | solution.py:20
  368.3 6.3 %collective-permute-start.84 = (f32[2,1,2,16]{3,2,1,0:T(2,128)S(1)}, f32[2,1,2,16]{3,2,1,0:T(2,128)S(1)}, u32[]{:S(2)}, u32[]{:S(2)}) collective-permute-start(f32[2,1,2,16]{3,2,1,0:T(2,128)S(1)} %get-tuple-element.173), channel_id=1, source_target_pairs={{8,0},{16,8},{24,16},{9,1},{17,9},{25,17},{10,2},{18,10},{26,18},{... | collective-permute-start | bytes 776 | tf_op jit(solution)/shard_map/ppermute | solution.py:23
  384.0 6.0 %collective-permute-start.89 = (f32[2,4,4,1]{3,2,1,0:T(4,128)S(1)}, f32[2,4,4,1]{3,2,1,0:T(4,128)S(1)}, u32[]{:S(2)}, u32[]{:S(2)}) collective-permute-start(f32[2,4,4,1]{3,2,1,0:T(4,128)S(1)} %get-tuple-element.125), channel_id=1, source_target_pairs={{0,1},{1,2},{2,3},{4,5},{5,6},{6,7},{8,9},{9,10},{10,11},{12,13},{... | collective-permute-start | bytes 392 | tf_op jit(solution)/shard_map/ppermute | solution.py:20
  390.4 6.3 %collective-permute-start.90 = (f32[2,1,4,32]{3,2,1,0:T(4,128)S(1)}, f32[2,1,4,32]{3,2,1,0:T(4,128)S(1)}, u32[]{:S(2)}, u32[]{:S(2)}) collective-permute-start(f32[2,1,4,32]{3,2,1,0:T(4,128)S(1)} %get-tuple-element.122), channel_id=1, source_target_pairs={{8,0},{16,8},{24,16},{9,1},{17,9},{25,17},{10,2},{18,10},{26,18},{... | collective-permute-start | bytes 3080 | tf_op jit(solution)/shard_map/ppermute | solution.py:23
  404.8 6.0 %collective-permute-start.94 = (f32[2,6,6,1]{3,2,1,0:T(8,128)S(1)}, f32[2,6,6,1]{3,2,1,0:T(8,128)S(1)}, u32[]{:S(2)}, u32[]{:S(2)}) collective-permute-start(f32[2,6,6,1]{3,2,1,0:T(8,128)S(1)} %get-tuple-element.96), channel_id=1, source_target_pairs={{1,0},{2,1},{3,2},{5,4},{6,5},{7,6},{9,8},{10,9},{11,10},{13,12},{... | collective-permute-start | bytes 872 | tf_op jit(solution)/shard_map/ppermute | solution.py:23
  406.1 6.3 %collective-permute-start.95 = (f32[2,6,6,1]{3,2,1,0:T(8,128)S(1)}, f32[2,6,6,1]{3,2,1,0:T(8,128)S(1)}, u32[]{:S(2)}, u32[]{:S(2)}) collective-permute-start(f32[2,6,6,1]{3,2,1,0:T(8,128)S(1)} %get-tuple-element.97), channel_id=1, source_target_pairs={{0,1},{1,2},{2,3},{4,5},{5,6},{6,7},{8,9},{9,10},{10,11},{12,13},{... | collective-permute-start | bytes 872 | tf_op jit(solution)/shard_map/ppermute | solution.py:20
  412.6 6.3 %collective-permute-start.96 = (f32[2,1,4,32]{3,2,1,0:T(4,128)S(1)}, f32[2,1,4,32]{3,2,1,0:T(4,128)S(1)}, u32[]{:S(2)}, u32[]{:S(2)}) collective-permute-start(f32[2,1,4,32]{3,2,1,0:T(4,128)S(1)} %get-tuple-element.120), channel_id=1, source_target_pairs={{8,0},{16,8},{24,16},{9,1},{17,9},{25,17},{10,2},{18,10},{26,18},{... | collective-permute-start | bytes 3080 | tf_op jit(solution)/shard_map/ppermute | solution.py:23
  427.1 6.0 %collective-permute-start.100 = (f32[2,6,6,1]{3,2,1,0:T(8,128)S(1)}, f32[2,6,6,1]{3,2,1,0:T(8,128)S(1)}, u32[]{:S(2)}, u32[]{:S(2)}) collective-permute-start(f32[2,6,6,1]{3,2,1,0:T(8,128)S(1)} %get-tuple-element.94), channel_id=1, source_target_pairs={{1,0},{2,1},{3,2},{5,4},{6,5},{7,6},{9,8},{10,9},{11,10},{13,12},{... | collective-permute-start | bytes 872 | tf_op jit(solution)/shard_map/ppermute | solution.py:23
  428.4 6.3 %collective-permute-start.101 = (f32[2,6,6,1]{3,2,1,0:T(8,128)S(1)}, f32[2,6,6,1]{3,2,1,0:T(8,128)S(1)}, u32[]{:S(2)}, u32[]{:S(2)}) collective-permute-start(f32[2,6,6,1]{3,2,1,0:T(8,128)S(1)} %get-tuple-element.95), channel_id=1, source_target_pairs={{0,1},{1,2},{2,3},{4,5},{5,6},{6,7},{8,9},{9,10},{10,11},{12,13},{... | collective-permute-start | bytes 872 | tf_op jit(solution)/shard_map/ppermute | solution.py:20
  437.0 6.3 %collective-permute-start.102 = (f32[2,1,8,64]{3,2,1,0:T(8,128)S(1)}, f32[2,1,8,64]{3,2,1,0:T(8,128)S(1)}, u32[]{:S(2)}, u32[]{:S(2)}) collective-permute-start(f32[2,1,8,64]{3,2,1,0:T(8,128)S(1)} %get-tuple-element.79), channel_id=1, source_target_pairs={{8,0},{16,8},{24,16},{9,1},{17,9},{25,17},{10,2},{18,10},{26,18},{... | collective-permute-start | bytes 12296 | tf_op jit(solution)/shard_map/ppermute | solution.py:23
  445.5 5.9 %collective-permute-start.105 = (f32[2,10,1,64]{3,2,1,0:T(1,128)S(1)}, f32[2,10,1,64]{3,2,1,0:T(1,128)S(1)}, u32[]{:S(2)}, u32[]{:S(2)}) collective-permute-start(f32[2,10,1,64]{3,2,1,0:T(1,128)S(1)} %get-tuple-element.71), channel_id=1, source_target_pairs={{0,4},{1,5},{2,6},{3,7},{8,12},{9,13},{10,14},{11,15},{16,20},{17,... | collective-permute-start | bytes 15368 | tf_op jit(solution)/shard_map/ppermute | solution.py:20
  451.6 7.2 %collective-permute-start.106 = (f32[2,10,10,1]{3,2,1,0:T(8,128)S(1)}, f32[2,10,10,1]{3,2,1,0:T(8,128)S(1)}, u32[]{:S(2)}, u32[]{:S(2)}) collective-permute-start(f32[2,10,10,1]{3,2,1,0:T(8,128)S(1)} %get-tuple-element.55), channel_id=1, source_target_pairs={{1,0},{2,1},{3,2},{5,4},{6,5},{7,6},{9,8},{10,9},{11,10},{13,12},{... | collective-permute-start | bytes 2408 | tf_op jit(solution)/shard_map/ppermute | solution.py:23
  452.9 7.4 %collective-permute-start.107 = (f32[2,10,10,1]{3,2,1,0:T(8,128)S(1)}, f32[2,10,10,1]{3,2,1,0:T(8,128)S(1)}, u32[]{:S(2)}, u32[]{:S(2)}) collective-permute-start(f32[2,10,10,1]{3,2,1,0:T(8,128)S(1)} %get-tuple-element.56), channel_id=1, source_target_pairs={{0,1},{1,2},{2,3},{4,5},{5,6},{6,7},{8,9},{9,10},{10,11},{12,13},{... | collective-permute-start | bytes 2408 | tf_op jit(solution)/shard_map/ppermute | solution.py:20
  460.6 6.4 %collective-permute-start.108 = (f32[2,1,8,64]{3,2,1,0:T(8,128)S(1)}, f32[2,1,8,64]{3,2,1,0:T(8,128)S(1)}, u32[]{:S(2)}, u32[]{:S(2)}) collective-permute-start(f32[2,1,8,64]{3,2,1,0:T(8,128)S(1)} %get-tuple-element.77), channel_id=1, source_target_pairs={{8,0},{16,8},{24,16},{9,1},{17,9},{25,17},{10,2},{18,10},{26,18},{... | collective-permute-start | bytes 12296 | tf_op jit(solution)/shard_map/ppermute | solution.py:23
  469.1 5.9 %collective-permute-start.111 = (f32[2,10,1,64]{3,2,1,0:T(1,128)S(1)}, f32[2,10,1,64]{3,2,1,0:T(1,128)S(1)}, u32[]{:S(2)}, u32[]{:S(2)}) collective-permute-start(f32[2,10,1,64]{3,2,1,0:T(1,128)S(1)} %get-tuple-element.69), channel_id=1, source_target_pairs={{0,4},{1,5},{2,6},{3,7},{8,12},{9,13},{10,14},{11,15},{16,20},{17,... | collective-permute-start | bytes 15368 | tf_op jit(solution)/shard_map/ppermute | solution.py:20
  475.1 7.4 %collective-permute-start.112 = (f32[2,10,10,1]{3,2,1,0:T(8,128)S(1)}, f32[2,10,10,1]{3,2,1,0:T(8,128)S(1)}, u32[]{:S(2)}, u32[]{:S(2)}) collective-permute-start(f32[2,10,10,1]{3,2,1,0:T(8,128)S(1)} %get-tuple-element.53), channel_id=1, source_target_pairs={{1,0},{2,1},{3,2},{5,4},{6,5},{7,6},{9,8},{10,9},{11,10},{13,12},{... | collective-permute-start | bytes 2408 | tf_op jit(solution)/shard_map/ppermute | solution.py:23
  476.4 7.5 %collective-permute-start.113 = (f32[2,10,10,1]{3,2,1,0:T(8,128)S(1)}, f32[2,10,10,1]{3,2,1,0:T(8,128)S(1)}, u32[]{:S(2)}, u32[]{:S(2)}) collective-permute-start(f32[2,10,10,1]{3,2,1,0:T(8,128)S(1)} %get-tuple-element.54), channel_id=1, source_target_pairs={{0,1},{1,2},{2,3},{4,5},{5,6},{6,7},{8,9},{9,10},{10,11},{12,13},{... | collective-permute-start | bytes 2408 | tf_op jit(solution)/shard_map/ppermute | solution.py:20
  503.5 6.4 %collective-permute-start.114 = (f32[2,1,16,128]{3,2,1,0:T(8,128)S(1)}, f32[2,1,16,128]{3,2,1,0:T(8,128)S(1)}, u32[]{:S(2)}, u32[]{:S(2)}) collective-permute-start(f32[2,1,16,128]{3,2,1,0:T(8,128)S(1)} %get-tuple-element.39), channel_id=1, source_target_pairs={{8,0},{16,8},{24,16},{9,1},{17,9},{25,17},{10,2},{18,10},{26,18},{... | collective-permute-start | bytes 49160 | tf_op jit(solution)/shard_map/ppermute | solution.py:23
  504.8 5.9 %collective-permute-start.115 = (f32[2,1,16,128]{3,2,1,0:T(8,128)S(1)}, f32[2,1,16,128]{3,2,1,0:T(8,128)S(1)}, u32[]{:S(2)}, u32[]{:S(2)}) collective-permute-start(f32[2,1,16,128]{3,2,1,0:T(8,128)S(1)} %get-tuple-element.40), channel_id=1, source_target_pairs={{0,8},{8,16},{16,24},{1,9},{9,17},{17,25},{2,10},{10,18},{18,26},{... | collective-permute-start | bytes 49160 | tf_op jit(solution)/shard_map/ppermute | solution.py:20
  512.1 6.0 %collective-permute-start.117 = (f32[2,18,1,128]{3,2,1,0:T(1,128)S(1)}, f32[2,18,1,128]{3,2,1,0:T(1,128)S(1)}, u32[]{:S(2)}, u32[]{:S(2)}) collective-permute-start(f32[2,18,1,128]{3,2,1,0:T(1,128)S(1)} %get-tuple-element.31), channel_id=1, source_target_pairs={{0,4},{1,5},{2,6},{3,7},{8,12},{9,13},{10,14},{11,15},{16,20},{17,... | collective-permute-start | bytes 55304 | tf_op jit(solution)/shard_map/ppermute | solution.py:20
  518.3 12.3 %collective-permute-start.118 = (f32[2,18,18,1]{3,2,1,0:T(8,128)S(1)}, f32[2,18,18,1]{3,2,1,0:T(8,128)S(1)}, u32[]{:S(2)}, u32[]{:S(2)}) collective-permute-start(f32[2,18,18,1]{3,2,1,0:T(8,128)S(1)} %get-tuple-element.15), channel_id=1, source_target_pairs={{1,0},{2,1},{3,2},{5,4},{6,5},{7,6},{9,8},{10,9},{11,10},{13,12},{... | collective-permute-start | bytes 7784 | tf_op jit(solution)/shard_map/ppermute | solution.py:23
  519.6 12.7 %collective-permute-start.119 = (f32[2,18,18,1]{3,2,1,0:T(8,128)S(1)}, f32[2,18,18,1]{3,2,1,0:T(8,128)S(1)}, u32[]{:S(2)}, u32[]{:S(2)}) collective-permute-start(f32[2,18,18,1]{3,2,1,0:T(8,128)S(1)} %get-tuple-element.16), channel_id=1, source_target_pairs={{0,1},{1,2},{2,3},{4,5},{5,6},{6,7},{8,9},{9,10},{10,11},{12,13},{... | collective-permute-start | bytes 7784 | tf_op jit(solution)/shard_map/ppermute | solution.py:20
  533.0 6.5 %collective-permute-start.120 = (f32[2,1,16,128]{3,2,1,0:T(8,128)S(1)}, f32[2,1,16,128]{3,2,1,0:T(8,128)S(1)}, u32[]{:S(2)}, u32[]{:S(2)}) collective-permute-start(f32[2,1,16,128]{3,2,1,0:T(8,128)S(1)} %get-tuple-element.37), channel_id=1, source_target_pairs={{8,0},{16,8},{24,16},{9,1},{17,9},{25,17},{10,2},{18,10},{26,18},{... | collective-permute-start | bytes 49160 | tf_op jit(solution)/shard_map/ppermute | solution.py:23
  534.3 6.0 %collective-permute-start.121 = (f32[2,1,16,128]{3,2,1,0:T(8,128)S(1)}, f32[2,1,16,128]{3,2,1,0:T(8,128)S(1)}, u32[]{:S(2)}, u32[]{:S(2)}) collective-permute-start(f32[2,1,16,128]{3,2,1,0:T(8,128)S(1)} %get-tuple-element.38), channel_id=1, source_target_pairs={{0,8},{8,16},{16,24},{1,9},{9,17},{17,25},{2,10},{10,18},{18,26},{... | collective-permute-start | bytes 49160 | tf_op jit(solution)/shard_map/ppermute | solution.py:20
  541.7 6.0 %collective-permute-start.123 = (f32[2,18,1,128]{3,2,1,0:T(1,128)S(1)}, f32[2,18,1,128]{3,2,1,0:T(1,128)S(1)}, u32[]{:S(2)}, u32[]{:S(2)}) collective-permute-start(f32[2,18,1,128]{3,2,1,0:T(1,128)S(1)} %get-tuple-element.29), channel_id=1, source_target_pairs={{0,4},{1,5},{2,6},{3,7},{8,12},{9,13},{10,14},{11,15},{16,20},{17,... | collective-permute-start | bytes 55304 | tf_op jit(solution)/shard_map/ppermute | solution.py:20
  547.9 13.4 %collective-permute-start.124 = (f32[2,18,18,1]{3,2,1,0:T(8,128)S(1)}, f32[2,18,18,1]{3,2,1,0:T(8,128)S(1)}, u32[]{:S(2)}, u32[]{:S(2)}) collective-permute-start(f32[2,18,18,1]{3,2,1,0:T(8,128)S(1)} %get-tuple-element.13), channel_id=1, source_target_pairs={{1,0},{2,1},{3,2},{5,4},{6,5},{7,6},{9,8},{10,9},{11,10},{13,12},{... | collective-permute-start | bytes 7784 | tf_op jit(solution)/shard_map/ppermute | solution.py:23
  549.2 13.8 %collective-permute-start.125 = (f32[2,18,18,1]{3,2,1,0:T(8,128)S(1)}, f32[2,18,18,1]{3,2,1,0:T(8,128)S(1)}, u32[]{:S(2)}, u32[]{:S(2)}) collective-permute-start(f32[2,18,18,1]{3,2,1,0:T(8,128)S(1)} %get-tuple-element.14), channel_id=1, source_target_pairs={{0,1},{1,2},{2,3},{4,5},{5,6},{6,7},{8,9},{9,10},{10,11},{12,13},{... | collective-permute-start | bytes 7784 | tf_op jit(solution)/shard_map/ppermute | solution.py:20
  (86 other events, 1071.0 us)
where the time goes:
time: 571 us; the launch traced here: 564 us
  starting transfers between devices  370 us (65%)
  waiting for transfers between devices  109 us (19%)
  local copies, waits for them, and re-layouts  60.1 us (11%)
  other arithmetic  22.3 us (4%)
    ppermute x63, starting transfers between devices, extended(): lax.ppermute(lax.slice_in_dim(block, block.shape[dim] - width, None, axis...  288 us
    ppermute x63, starting transfers between devices, extended(): lax.ppermute(lax.slice_in_dim(block, 0, width, axis=dim), axis, backward)  81.4 us
    ppermute x63, waiting for transfers between devices, extended(): lax.ppermute(lax.slice_in_dim(block, block.shape[dim] - width, None, axis...  72 us
    ppermute x63, waiting for transfers between devices, extended(): lax.ppermute(lax.slice_in_dim(block, 0, width, axis=dim), axis, backward)  37.4 us
    reshape x2, local copies, waits for them, and re-layouts, restrict(): values.reshape(leading + (first_length // 2, 2, second_length // 2, 2, th...  27.7 us
    reshape x3, local copies, waits for them, and re-layouts, prolong(): expanded.reshape(leading + (2 * first_length, 2 * second_length, 2 * thir...  14.5 us
    reduce_sum x10, other arithmetic, restrict(): grouped.mean(axis=(leading_rank + 1, leading_rank + 3, leading_rank + 5))  13.2 us
  transfers between devices with their start and end apart: 126, of which 73 were waited for; matrix products, arithmetic and copies ran while one was open for 3% of the time, Pallas kernels for 0%

commit v1 on v0

v1 whole, which is shorter than its diff:
```python
import functools

import jax
import jax.numpy as jnp
from jax import lax
from jax.experimental import pallas as pl
from jax.experimental.pallas import tpu as pltpu
from jax.sharding import PartitionSpec as P

MESH = pl.DeviceIdType.MESH
AXES = ("gx", "gy", "gz")
COARSE_SWEEPS = 6
WAVE = 0.25
WAVE2 = 0.0625
LANES = 128


def lane_of(shape):
    return lax.broadcasted_iota(jnp.int32, shape, len(shape) - 1)


def row_of(shape):
    return lax.broadcasted_iota(jnp.int32, shape, len(shape) - 2)


def roll(value, shift, axis):
    if isinstance(shift, int):
        shift %= value.shape[axis]
        if shift == 0:
            return value
    return pltpu.roll(value, shift, axis)


def coefficients(mach, level):
    scale = 0.25**level
    axial = scale * (1.0 - mach * mach)
    real = 2.0 * axial + (4.0 * scale - WAVE2)
    imaginary = 0.5 * WAVE2
    half = 0.5 / (real * real + imaginary * imaginary)
    return axial, real * half, -imaginary * half


def pair_sum(value, rows, lanes):
    shape = value.shape
    even = (row_of(shape) // rows) % 2 == 0
    value = value + jnp.where(even, roll(value, shape[0] - rows, 0), roll(value, rows, 0))
    even = (lane_of(shape) // lanes) % 2 == 0
    return value + jnp.where(even, roll(value, LANES - lanes, 1), roll(value, lanes, 1))


def kernel(sizes, g0, mach_in, out, v0, v1, gl1, co0, co1, ys0, yr0, ys1, yr1, zs, zr, gm, gg,
           va, vb, vc, gc2, gc3, gc4, cc2, cc3, cc4, own, send_sem, recv_sem, gs_sem, gr_sem):
    nx, ny, nz = sizes
    count = nx * ny * nz
    ix, iy, iz = (lax.axis_index(a) for a in AXES)
    me = (ix * ny + iy) * nz + iz
    X0, Y0 = g0.shape[1], g0.shape[2]
    tile = (Y0, LANES)
    here = {"gx": ix, "gy": iy, "gz": iz}
    size = dict(zip(AXES, sizes))
    yall = va.shape[3]
    XC = X0 // 4

    def peer(d):
        t = lax.rem(me + d, count)
        return (t // (ny * nz), lax.rem(t // nz, ny), lax.rem(t, nz))

    barrier = pltpu.get_barrier_semaphore()

    def greet(d, carry):
        pl.semaphore_signal(barrier, inc=1, device_id=peer(d), device_id_type=MESH)
        return carry

    for ref in (v0, v1):
        zero = jnp.zeros((2,) + tile, jnp.float32)
        for r in range(4):
            ref[r, :, 0] = zero
            ref[r, :, ref.shape[2] - 1] = zero
    yr0[...] = jnp.zeros(yr0.shape, jnp.float32)
    yr1[...] = jnp.zeros(yr1.shape, jnp.float32)
    zr[...] = jnp.zeros(zr.shape, jnp.float32)
    lax.fori_loop(1, count, greet, 0)

    lane, row = lane_of(tile), row_of(tile)
    levels = (
        dict(v=v0, g=g0, co=co0, ys=ys0, yr=yr0, X=X0, w=1, l=0),
        dict(v=v1, g=gl1, co=co1, ys=ys1, yr=yr1, X=X0 // 2, w=2, l=1),
    )

    def links(L, r):
        X, v, ys, yr = L["X"], L["v"].at[r], L["ys"].at[r], L["yr"].at[r]
        k = 4 * L["l"] + r
        pieces = []
        for n, (axis, step, src, dst) in enumerate((
            ("gz", 1, zs.at[k], zr.at[k, 0]),
            ("gz", -1, zs.at[k], zr.at[k, 1]),
            ("gy", 1, ys.at[1], yr.at[0]),
            ("gy", -1, ys.at[0], yr.at[1]),
            ("gx", 1, v.at[:, X], v.at[:, 0]),
            ("gx", -1, v.at[:, 1], v.at[:, X + 1]),
        )):
            at = here[axis]
            up, down = at < size[axis] - 1, at > 0
            to = tuple(here[a] + step if a == axis else here[a] for a in AXES)
            copy = pltpu.make_async_remote_copy(
                src_ref=src, dst_ref=dst, send_sem=send_sem.at[k, n], recv_sem=recv_sem.at[k, n],
                device_id=to, device_id_type=MESH,
            )
            pieces.append((copy, up if step > 0 else down, down if step > 0 else up))
        return pieces

    def start(L, r):
        for copy, sends, _ in links(L, r):
            pl.when(sends)(copy.start)

    def arrive(L, r):
        for copy, _, receives in links(L, r):
            pl.when(receives)(copy.wait_recv)

    def sent(L, r):
        for copy, sends, _ in links(L, r):
            pl.when(sends)(copy.wait_send)

    def put(L, r, x, values, packed):
        v, ys = L["v"], L["ys"]
        for c in range(2):
            value = values[c]
            v[r, c, x + 1] = value
            ys[r, 0, c, pl.ds(x, 1), :] = value[:1]
            ys[r, 1, c, pl.ds(x, 1), :] = value[Y0 - 1:]
            packed = jnp.where(lane // 4 == x + 16 * c, roll(value, 4 * x + 2 + 64 * c, 1), packed)
        return packed

    def seal(L, r, packed):
        zs[4 * L["l"] + r] = packed
        start(L, r)

    def sides(L, r):
        k, w = 4 * L["l"] + r, L["w"]
        below = (lane % 4 >= 2 - w) & (lane % 4 < 2)
        return jnp.where(below, zr[k, 0], roll(zr[k, 1], LANES - 2 * w, 1))

    def terms(L, r, x, side):
        v, yr, w, co = L["v"], L["yr"], L["w"], L["co"]
        scale = 0.25 ** L["l"]
        axial, drift = co[0, x], co[3, x]
        centre, along, across = [], [], []
        slope = []
        for c in range(2):
            here_ = v[r, c, x + 1]
            east, west = v[r, c, x + 2], v[r, c, x]
            shift = lax.rem(4 * LANES - (4 * x + 2 - w + 64 * c), LANES)
            edge = roll(side, shift, 1)
            lower = jnp.where(lane < w, edge, roll(here_, w, 1))
            upper = jnp.where(lane >= LANES - w, edge, roll(here_, LANES - w, 1))
            south = jnp.where(row < w, yr[r, 0, c, pl.ds(x, 1), :], roll(here_, w, 0))
            north = jnp.where(row >= Y0 - w, yr[r, 1, c, pl.ds(x, 1), :], roll(here_, Y0 - w, 0))
            centre.append(here_)
            across.append((lower + upper) + (south + north))
            along.append(east + west)
            slope.append(east - west)
        if L["l"]:
            across = [scale * a for a in across]
        g = L["g"]
        real = g[0, x] + axial * along[0] + across[0] - drift * slope[1]
        imaginary = g[1, x] + axial * along[1] + across[1] + drift * slope[0]
        return centre, (real, imaginary)

    def relaxed(centre, t, hr, hi):
        return (0.5 * centre[0] + (hr * t[0] - hi * t[1]), 0.5 * centre[1] + (hi * t[0] + hr * t[1]))

    def residue(centre, t, axial, scale):
        dr = 2.0 * axial + (4.0 * scale - WAVE2)
        di = 0.5 * WAVE2
        return (t[0] - dr * centre[0] + di * centre[1], t[1] - dr * centre[1] - di * centre[0])

    def relax(L, r):
        arrive(L, r)
        side = sides(L, r)
        co = L["co"]

        def body(x, packed):
            centre, t = terms(L, r, x, side)
            return put(L, r + 1, x, relaxed(centre, t, co[1, x], co[2, x]), packed)

        seal(L, r + 1, lax.fori_loop(0, L["X"], body, jnp.zeros(tile, jnp.float32), unroll=4))

    def last(L, r, store):
        arrive(L, r)
        side = sides(L, r)
        co = L["co"]

        def body(x, carry):
            centre, t = terms(L, r, x, side)
            store(x, relaxed(centre, t, co[1, x], co[2, x]))
            return carry

        lax.fori_loop(0, L["X"], body, 0, unroll=4)

    def residual(L, r, x, side):
        centre, t = terms(L, r, x, side)
        return residue(centre, t, L["co"][0, x], 0.25 ** L["l"])

    def set_coefficients(co, x, mach, level):
        axial, hr, hi = coefficients(mach, level)
        co[0, x] = axial
        co[1, x] = hr
        co[2, x] = hi
        co[3, x] = (WAVE * 0.5**level) * mach
        return hr, hi

    def first(hr, hi, gr, gi):
        return hr * gr - hi * gi, hr * gi + hi * gr

    fine, half = levels

    def open_plane(x, packed):
        mach = mach_in[x].astype(jnp.float32)
        hr, hi = set_coefficients(co0, x, mach, 0)
        return put(fine, 0, x, first(hr, hi, g0[0, x], g0[1, x]), packed)

    packed = lax.fori_loop(0, X0, open_plane, jnp.zeros(tile, jnp.float32), unroll=4)

    def mach_plane(x, carry):
        mach = mach_in[2 * x].astype(jnp.float32) + mach_in[2 * x + 1].astype(jnp.float32)
        set_coefficients(co1, x, 0.125 * pair_sum(mach, 1, 1), 1)
        return carry

    pl.semaphore_wait(barrier, count - 1)
    seal(fine, 0, packed)

    lax.fori_loop(0, X0 // 2, mach_plane, 0, unroll=2)
    undo = 1.0 / (WAVE * 0.5)
    group = jnp.zeros(tile, jnp.float32)
    for x in range(XC):
        mach = pair_sum((co1[3, 2 * x] + co1[3, 2 * x + 1]) * undo, 2, 2) * 0.125
        group = jnp.where(lane % 4 == x, mach, group)
    for y in range(4):
        gm[me, y:y + 1, :] = group[4 * y:4 * y + 1]
        gm[me, y + 4:y + 5, :] = group[4 * y:4 * y + 1]

    def tell(ref, n):
        def one(d, carry):
            pltpu.make_async_remote_copy(
                src_ref=ref.at[me], dst_ref=ref.at[me], send_sem=gs_sem.at[n], recv_sem=gr_sem.at[n],
                device_id=peer(d), device_id_type=MESH,
            ).start()
            return carry

        lax.fori_loop(1, count, one, 0)

    def bulk(ref, n):
        part = ref.at[pl.ds(0, count - 1)]
        return pltpu.make_async_remote_copy(
            src_ref=part, dst_ref=part, send_sem=gs_sem.at[n], recv_sem=gr_sem.at[n],
            device_id=peer(1), device_id_type=MESH,
        )

    def spread(ref, store):
        lane8 = lane_of((8, LANES))

        def block(bx, carry):
            for by in range(ny):
                tiles = [ref[(bx * ny + by) * nz + bz] for bz in range(nz)]
                for x in range(XC):
                    value = tiles[0]
                    for bz in range(nz):
                        moved = roll(tiles[bz], bz - x, 1)
                        value = moved if bz == 0 else jnp.where(lane8 % 4 == bz, moved, value)
                    store(bx * XC + x, by, value)
            return carry

        lax.fori_loop(0, nx, block, 0)

    tell(gm, 0)

    wide = (yall, LANES)
    clane, crow = lane_of(wide), row_of(wide)
    coarse = (
        dict(v=va, g=gc2, co=cc2, w=1, l=2),
        dict(v=vb, g=gc3, co=cc3, w=2, l=3),
        dict(v=vc, g=gc4, co=cc4, w=4, l=4),
    )
    for C in coarse:
        v = C["v"]
        C["X"] = v.shape[2] - 2
        C["unroll"] = min(4, C["X"])
        for r in range(2):
            for c in range(2):
                v[r, c, 0] = jnp.zeros(wide, jnp.float32)
                v[r, c, C["X"] + 1] = jnp.zeros(wide, jnp.float32)

    def over(C, body):
        def step(x, carry):
            body(x)
            return carry

        lax.fori_loop(0, C["X"], step, 0, unroll=C["unroll"])

    def coarse_terms(C, r, x):
        v, w, co, g = C["v"], C["w"], C["co"], C["g"]
        m = 4 * w
        scale = 0.25 ** C["l"]
        top = clane >= LANES - m
        centre, along, across, slope = [], [], [], []
        for c in range(2):
            value = v[r, c, x + 1]
            east, west = v[r, c, x + 2], v[r, c, x]
            upper = jnp.where(top, roll(value, LANES - m - 1, 1), roll(value, LANES - m, 1))
            upper = jnp.where(top & (clane % 4 == 3), 0.0, upper)
            lower = jnp.where(clane < m, roll(value, m + 1, 1), roll(value, m, 1))
            lower = jnp.where((clane < m) & (clane % 4 == 0), 0.0, lower)
            south = jnp.where(crow < w, 0.0, roll(value, w, 0))
            north = jnp.where(crow >= yall - w, 0.0, roll(value, yall - w, 0))
            centre.append(value)
            across.append(scale * ((lower + upper) + (south + north)))
            along.append(east + west)
            slope.append(east - west)
        real = g[0, x] + co[0, x] * along[0] + across[0] - co[3, x] * slope[1]
        imaginary = g[1, x] + co[0, x] * along[1] + across[1] + co[3, x] * slope[0]
        return centre, (real, imaginary)

    def coarse_first(C):
        def body(x):
            g, co = C["g"], C["co"]
            values = first(co[1, x], co[2, x], g[0, x], g[1, x])
            for c in range(2):
                C["v"][0, c, x + 1] = values[c]

        over(C, body)

    def coarse_relax(C, r):
        def body(x):
            centre, t = coarse_terms(C, r, x)
            values = relaxed(centre, t, C["co"][1, x], C["co"][2, x])
            for c in range(2):
                C["v"][1 - r, c, x + 1] = values[c]

        over(C, body)

    def coarse_down(C, D, r):
        w = C["w"]

        def body(x):
            total = None
            for half_ in range(2):
                centre, t = coarse_terms(C, r, 2 * x + half_)
                res = residue(centre, t, C["co"][0, 2 * x + half_], 0.25 ** C["l"])
                total = res if total is None else tuple(a + b for a, b in zip(total, res))
            for c in range(2):
                D["g"][c, x] = 0.125 * pair_sum(total[c], w, 4 * w)

        over(D, body)

    def coarse_up(C, D, r, rd):
        def body(x):
            for c in range(2):
                add = D["v"][rd, c, x + 1]
                for half_ in range(2):
                    C["v"][r, c, 2 * x + half_ + 1] = C["v"][r, c, 2 * x + half_ + 1] + add

        over(D, body)

    relax(fine, 0)
    arrive(fine, 1)
    side = sides(fine, 1)

    def down_plane(x, packed):
        a = residual(fine, 1, 2 * x, side)
        b = residual(fine, 1, 2 * x + 1, side)
        g = [0.125 * pair_sum(a[c] + b[c], 1, 1) for c in range(2)]
        for c in range(2):
            gl1[c, x] = g[c]
        return put(half, 0, x, first(co1[1, x], co1[2, x], g[0], g[1]), packed)

    packed = lax.fori_loop(0, X0 // 2, down_plane, jnp.zeros(tile, jnp.float32), unroll=2)
    seal(half, 0, packed)

    bulk(gm, 0).wait_recv()

    def store_mach(x, by, value):
        cc2[3, x, 4 * by:4 * by + 4, :] = value[:4]

    spread(gm, store_mach)
    over(coarse[0], lambda x: set_coefficients(cc2, x, cc2[3, x], 2))
    for C, D in zip(coarse[:-1], coarse[1:]):
        factor = 0.125 / (WAVE * 0.5 ** C["l"])

        def body(x, C=C, D=D, factor=factor):
            mach = factor * pair_sum(C["co"][3, 2 * x] + C["co"][3, 2 * x + 1], C["w"], 4 * C["w"])
            set_coefficients(D["co"], x, mach, D["l"])

        over(D, body)

    relax(half, 0)
    arrive(half, 1)
    side = sides(half, 1)
    groups = [jnp.zeros(tile, jnp.float32) for _ in range(2)]
    for x in range(XC):
        a = residual(half, 1, 2 * x, side)
        b = residual(half, 1, 2 * x + 1, side)
        for c in range(2):
            groups[c] = jnp.where(lane % 4 == x, 0.125 * pair_sum(a[c] + b[c], 2, 2), groups[c])
    for c in range(2):
        for y in range(4):
            gg[me, 4 * c + y:4 * c + y + 1, :] = groups[c][4 * y:4 * y + 1]
    tell(gg, 1)
    bulk(gg, 1).wait_recv()

    def store_source(x, by, value):
        for c in range(2):
            gc2[c, x, 4 * by:4 * by + 4, :] = value[4 * c:4 * c + 4]

    spread(gg, store_source)

    for C, D in zip(coarse[:-1], coarse[1:]):
        coarse_first(C)
        coarse_relax(C, 0)
        coarse_down(C, D, 1)
    coarse_first(coarse[2])
    at = 0
    for _ in range(COARSE_SWEEPS - 1):
        coarse_relax(coarse[2], at)
        at = 1 - at
    for C, D in ((coarse[1], coarse[2]), (coarse[0], coarse[1])):
        coarse_up(C, D, 1, at)
        coarse_relax(C, 1)
        coarse_relax(C, 0)
        at = 1

    packed = jnp.zeros(tile, jnp.float32)
    for x in range(XC):
        for c in range(2):
            value = va[1, c, ix * XC + x + 1]
            only = jnp.where(clane % 4 == iz, value, 0.0)
            back = only + roll(only, 1, 1)
            back = back + roll(back, 2, 1)
            ahead = only + roll(only, LANES - 1, 1)
            ahead = ahead + roll(ahead, LANES - 2, 1)
            own[c, x] = jnp.where(clane % 4 <= iz, ahead, back)
    for x in range(XC):
        add = []
        for c in range(2):
            value = own[c, x, pl.ds(4 * iy, 1), :]
            full = jnp.broadcast_to(value, tile)
            for y in range(1, 4):
                value = own[c, x, pl.ds(4 * iy + y, 1), :]
                full = jnp.where(row >= 4 * y, value, full)
            add.append(full)
        for half_ in range(2):
            values = [v1[1, c, 2 * x + half_ + 1] + add[c] for c in range(2)]
            packed = put(half, 2, 2 * x + half_, values, packed)
    seal(half, 2, packed)
    relax(half, 2)

    def store_half(x, values):
        for c in range(2):
            gl1[c, x] = values[c]

    last(half, 3, store_half)

    def up_plane(x, packed):
        values = [v0[1, c, x + 1] + gl1[c, x // 2] for c in range(2)]
        return put(fine, 2, x, values, packed)

    seal(fine, 2, lax.fori_loop(0, X0, up_plane, jnp.zeros(tile, jnp.float32), unroll=4))
    relax(fine, 2)

    def store_out(x, values):
        for c in range(2):
            out[c, x] = values[c]

    last(fine, 3, store_out)

    for r in range(4):
        sent(fine, r)
        sent(half, r)
    bulk(gm, 0).wait_send()
    bulk(gg, 1).wait_send()


def solution(mesh):
    sizes = tuple(mesh.shape[a] for a in AXES)
    nx, ny, nz = sizes
    count = nx * ny * nz

    def shards(source, mach):
        _, X, Y, Z = source.shape
        assert X == 16 and Y == 16 and Z == LANES and nz == 4, "unsupported sizes"
        f32 = jnp.float32
        yall = ny * Y // 4
        xs = [nx * X // 2**l for l in (2, 3, 4)]
        scratch = [
            pltpu.VMEM((4, 2, X + 2, Y, LANES), f32),
            pltpu.VMEM((4, 2, X // 2 + 2, Y, LANES), f32),
            pltpu.VMEM((2, X // 2, Y, LANES), f32),
            pltpu.VMEM((4, X, Y, LANES), f32),
            pltpu.VMEM((4, X // 2, Y, LANES), f32),
            pltpu.VMEM((4, 2, 2, X, LANES), f32),
            pltpu.VMEM((4, 2, 2, X, LANES), f32),
            pltpu.VMEM((4, 2, 2, X // 2, LANES), f32),
            pltpu.VMEM((4, 2, 2, X // 2, LANES), f32),
            pltpu.VMEM((8, Y, LANES), f32),
            pltpu.VMEM((8, 2, Y, LANES), f32),
            pltpu.VMEM((count, 8, LANES), f32),
            pltpu.VMEM((count, 8, LANES), f32),
        ]
        scratch += [pltpu.VMEM((2, 2, n + 2, yall, LANES), f32) for n in xs]
        scratch += [pltpu.VMEM((2, n, yall, LANES), f32) for n in xs]
        scratch += [pltpu.VMEM((4, n, yall, LANES), f32) for n in xs]
        scratch += [
            pltpu.VMEM((2, X // 4, yall, LANES), f32),
            pltpu.SemaphoreType.DMA((8, 6)),
            pltpu.SemaphoreType.DMA((8, 6)),
            pltpu.SemaphoreType.DMA((2,)),
            pltpu.SemaphoreType.DMA((2,)),
        ]
        return pl.pallas_call(
            functools.partial(kernel, sizes),
            out_shape=jax.ShapeDtypeStruct(source.shape, f32),
            in_specs=[pl.BlockSpec(memory_space=pltpu.VMEM)] * 2,
            out_specs=pl.BlockSpec(memory_space=pltpu.VMEM),
            scratch_shapes=scratch,
            compiler_params=pltpu.CompilerParams(
                collective_id=0, has_side_effects=True, vmem_limit_bytes=48 * 2**20
            ),
        )(source, mach)

    return jax.shard_map(
        shards,
        mesh=mesh,
        in_specs=(P(None, "gx", "gy", "gz"), P("gx", "gy", "gz")),
        out_specs=P(None, "gx", "gy", "gz"),
        check_vma=False,
    )
```

time: 571 us -> 46.9 us (0.08); the launches traced: 564 us -> 46.7 us
  starting transfers between devices: 370 us -> 0 us
  waiting for transfers between devices: 109 us -> 0 us
  local copies, waits for them, and re-layouts: 60.1 us -> 2.49 us
  Pallas kernels: 0 us -> 44.2 us
  other arithmetic: 22.3 us -> 0 us
    ppermute x126 -> x0, starting transfers between devices: 370 us -> none  [the longest x63 288 us: extended(): lax.ppermute(lax.slice_in_dim(block, block.shape[dim] - width, None, axis...]
    ppermute x126 -> x0, waiting for transfers between devices: 109 us -> none  [the longest x63 72 us: extended(): lax.ppermute(lax.slice_in_dim(block, block.shape[dim] - width, None, axis...]
    pallas_call x0 -> x1, Pallas kernels: none -> 44.2 us  [shards(): pl.pallas_call(functools.partial(kernel, sizes), out_shape=jax.ShapeDtype...]
    reshape x5 -> x0, local copies, waits for them, and re-layouts: 42.2 us -> none  [the longest x2 27.7 us: restrict(): values.reshape(leading + (first_length // 2, 2, second_length // 2, 2, th...]
    reduce_sum x10 -> x0, other arithmetic: 13.2 us -> none  [restrict(): grouped.mean(axis=(leading_rank + 1, leading_rank + 3, leading_rank + 5))]
    broadcast_in_dim x5 -> x0, local copies, waits for them, and re-layouts: 7.01 us -> none  [prolong(): jnp.broadcast_to(expanded, leading + (first_length, 2, second_length, 2,...]
  transfers between devices with their start and end apart: 126 -> 0, of which waited for: 73 -> 0; matrix products, arithmetic and copies ran while one was open for 3% -> 0% of each run, Pallas kernels for 0% -> 0%
where the time goes in v1:
time: 46.9 us; the launch traced here: 46.7 us
  Pallas kernels  44.2 us (94%)
  local copies, waits for them, and re-layouts  2.49 us (5%)
    pallas_call x1, Pallas kernels, shards(): pl.pallas_call(functools.partial(kernel, sizes), out_shape=jax.ShapeDtype...  44.2 us
    unnamed x5, local copies, waits for them, and re-layouts  2.49 us

profile of v1, /device:TPU:0, one launch (start us, length us, event | category | flops | bytes accessed | tf_op | source)
XLA Modules:
  0.0 46.7 jit_solution(17814874389966914743)
XLA Ops:
  0.0 0.0 copy-start
  0.0 0.9 %copy-done = f32[2,16,16,128]{3,2,1,0:T(8,128)S(1)} copy-done((f32[2,16,16,128]{3,2,1,0:T(8,128)S(1)}, f32[2,16,16,128]{3,2,1,0:T(8,128)}, u32[]{:S(2)}) %copy-start) | copy-done | bytes 262168
  1.0 0.0 copy-start.1
  1.0 0.8 %copy-done.1 = bf16[16,16,128]{2,1,0:T(8,128)(2,1)S(1)} copy-done((bf16[16,16,128]{2,1,0:T(8,128)(2,1)S(1)}, bf16[16,16,128]{2,1,0:T(8,128)(2,1)}, u32[]{:S(2)}) %copy-start.1) | copy-done | bytes 65560
  1.8 44.2 %shard_map.28 = f32[2,16,16,128]{3,2,1,0:T(8,128)S(1)} custom-call(f32[2,16,16,128]{3,2,1,0:T(8,128)S(1)} %copy-done, bf16[16,16,128]{2,1,0:T(8,128)(2,1)S(1)} %copy-done.1), custom_call_target="tpu_custom_call" | custom-call | tf_op jit(solution)/shard_map/pallas_call | solution.py:518
  46.0 0.7 %copy.4 = f32[2,16,16,128]{3,2,1,0:T(8,128)} copy(f32[2,16,16,128]{3,2,1,0:T(8,128)S(1)} %shard_map.28) | data formatting | bytes 524288
Async XLA Ops:
  0.0 0.9 %copy-start = (f32[2,16,16,128]{3,2,1,0:T(8,128)S(1)}, f32[2,16,16,128]{3,2,1,0:T(8,128)}, u32[]{:S(2)}) copy-start(f32[2,16,16,128]{3,2,1,0:T(8,128)} %g0.1) | copy-start | bytes 786436
  1.0 0.8 %copy-start.1 = (bf16[16,16,128]{2,1,0:T(8,128)(2,1)S(1)}, bf16[16,16,128]{2,1,0:T(8,128)(2,1)}, u32[]{:S(2)}) copy-start(bf16[16,16,128]{2,1,0:T(8,128)(2,1)} %mach_in.1) | copy-start | bytes 196612

commit v2 on v1

--- a/solution.py
+++ b/solution.py
@@ -48,7 +48,7 @@
     return value + jnp.where(even, roll(value, LANES - lanes, 1), roll(value, lanes, 1))
 
 
-def kernel(sizes, g0, mach_in, out, v0, v1, gl1, co0, co1, ys0, yr0, ys1, yr1, zs, zr, gm, gg,
+def kernel(sizes, g_hbm, mach_hbm, out, g0, mach_in, in_sem, v0, v1, gl1, co0, co1, ys0, yr0, ys1, yr1, zs, zr, gm, gg,
            va, vb, vc, gc2, gc3, gc4, cc2, cc3, cc4, own, send_sem, recv_sem, gs_sem, gr_sem):
     nx, ny, nz = sizes
     count = nx * ny * nz
@@ -65,6 +65,12 @@
         t = lax.rem(me + d, count)
         return (t // (ny * nz), lax.rem(t // nz, ny), lax.rem(t, nz))
 
+    loads = [
+        pltpu.make_async_copy(mach_hbm, mach_in, in_sem.at[0]),
+        pltpu.make_async_copy(g_hbm, g0, in_sem.at[1]),
+    ]
+    for load in loads:
+        load.start()
     barrier = pltpu.get_barrier_semaphore()
 
     def greet(d, carry):
@@ -113,7 +119,12 @@
         for copy, sends, _ in links(L, r):
             pl.when(sends)(copy.start)
 
+    flying = []
+
     def arrive(L, r):
+        for earlier in flying:
+            sent(*earlier)
+        flying[:] = [(L, r)]
         for copy, _, receives in links(L, r):
             pl.when(receives)(copy.wait_recv)
 
@@ -183,7 +194,7 @@
             centre, t = terms(L, r, x, side)
             return put(L, r + 1, x, relaxed(centre, t, co[1, x], co[2, x]), packed)
 
-        seal(L, r + 1, lax.fori_loop(0, L["X"], body, jnp.zeros(tile, jnp.float32), unroll=4))
+        seal(L, r + 1, lax.fori_loop(0, L["X"], body, jnp.zeros(tile, jnp.float32), unroll=True))
 
     def last(L, r, store):
         arrive(L, r)
@@ -195,7 +206,7 @@
             store(x, relaxed(centre, t, co[1, x], co[2, x]))
             return carry
 
-        lax.fori_loop(0, L["X"], body, 0, unroll=4)
+        lax.fori_loop(0, L["X"], body, 0, unroll=True)
 
     def residual(L, r, x, side):
         centre, t = terms(L, r, x, side)
@@ -219,7 +230,9 @@
         hr, hi = set_coefficients(co0, x, mach, 0)
         return put(fine, 0, x, first(hr, hi, g0[0, x], g0[1, x]), packed)
 
-    packed = lax.fori_loop(0, X0, open_plane, jnp.zeros(tile, jnp.float32), unroll=4)
+    for load in loads:
+        load.wait()
+    packed = lax.fori_loop(0, X0, open_plane, jnp.zeros(tile, jnp.float32), unroll=True)
 
     def mach_plane(x, carry):
         mach = mach_in[2 * x].astype(jnp.float32) + mach_in[2 * x + 1].astype(jnp.float32)
@@ -229,7 +242,7 @@
     pl.semaphore_wait(barrier, count - 1)
     seal(fine, 0, packed)
 
-    lax.fori_loop(0, X0 // 2, mach_plane, 0, unroll=2)
+    lax.fori_loop(0, X0 // 2, mach_plane, 0, unroll=True)
     undo = 1.0 / (WAVE * 0.5)
     group = jnp.zeros(tile, jnp.float32)
     for x in range(XC):
@@ -270,7 +283,7 @@
                     store(bx * XC + x, by, value)
             return carry
 
-        lax.fori_loop(0, nx, block, 0)
+        lax.fori_loop(0, nx, block, 0, unroll=True if nx <= 4 else 1)
 
     tell(gm, 0)
 
@@ -284,7 +297,7 @@
     for C in coarse:
         v = C["v"]
         C["X"] = v.shape[2] - 2
-        C["unroll"] = min(4, C["X"])
+        C["unroll"] = True if C["X"] <= 16 else 4
         for r in range(2):
             for c in range(2):
                 v[r, c, 0] = jnp.zeros(wide, jnp.float32)
@@ -373,7 +386,7 @@
             gl1[c, x] = g[c]
         return put(half, 0, x, first(co1[1, x], co1[2, x], g[0], g[1]), packed)
 
-    packed = lax.fori_loop(0, X0 // 2, down_plane, jnp.zeros(tile, jnp.float32), unroll=2)
+    packed = lax.fori_loop(0, X0 // 2, down_plane, jnp.zeros(tile, jnp.float32), unroll=True)
     seal(half, 0, packed)
 
     bulk(gm, 0).wait_recv()
@@ -405,6 +418,7 @@
         for y in range(4):
             gg[me, 4 * c + y:4 * c + y + 1, :] = groups[c][4 * y:4 * y + 1]
     tell(gg, 1)
+    bulk(gm, 0).wait_send()
     bulk(gg, 1).wait_recv()
 
     def store_source(x, by, value):
@@ -451,6 +465,7 @@
             values = [v1[1, c, 2 * x + half_ + 1] + add[c] for c in range(2)]
             packed = put(half, 2, 2 * x + half_, values, packed)
     seal(half, 2, packed)
+    bulk(gg, 1).wait_send()
     relax(half, 2)
 
     def store_half(x, values):
@@ -463,7 +478,7 @@
         values = [v0[1, c, x + 1] + gl1[c, x // 2] for c in range(2)]
         return put(fine, 2, x, values, packed)
 
-    seal(fine, 2, lax.fori_loop(0, X0, up_plane, jnp.zeros(tile, jnp.float32), unroll=4))
+    seal(fine, 2, lax.fori_loop(0, X0, up_plane, jnp.zeros(tile, jnp.float32), unroll=True))
     relax(fine, 2)
 
     def store_out(x, values):
@@ -472,11 +487,8 @@
 
     last(fine, 3, store_out)
 
-    for r in range(4):
-        sent(fine, r)
-        sent(half, r)
-    bulk(gm, 0).wait_send()
-    bulk(gg, 1).wait_send()
+    for earlier in flying:
+        sent(*earlier)
 
 
 def solution(mesh):
@@ -491,6 +503,9 @@
         yall = ny * Y // 4
         xs = [nx * X // 2**l for l in (2, 3, 4)]
         scratch = [
+            pltpu.VMEM(source.shape, f32),
+            pltpu.VMEM(mach.shape, mach.dtype),
+            pltpu.SemaphoreType.DMA((2,)),
             pltpu.VMEM((4, 2, X + 2, Y, LANES), f32),
             pltpu.VMEM((4, 2, X // 2 + 2, Y, LANES), f32),
             pltpu.VMEM((2, X // 2, Y, LANES), f32),
@@ -518,7 +533,7 @@
         return pl.pallas_call(
             functools.partial(kernel, sizes),
             out_shape=jax.ShapeDtypeStruct(source.shape, f32),
-            in_specs=[pl.BlockSpec(memory_space=pltpu.VMEM)] * 2,
+            in_specs=[pl.BlockSpec(memory_space=pl.ANY)] * 2,
             out_specs=pl.BlockSpec(memory_space=pltpu.VMEM),
             scratch_shapes=scratch,
             compiler_params=pltpu.CompilerParams(

time: 46.9 us -> 43.6 us (0.930)
  Pallas kernels: 44.2 us -> 40.9 us
    pallas_call x1, Pallas kernels: 44.2 us -> 40.9 us  [shards(): pl.pallas_call(functools.partial(kernel, sizes), out_shape=jax.ShapeDtype...]
where the time goes in v2:
time: 43.6 us; the launch traced here: 43.4 us
  Pallas kernels  40.9 us (94%)
  local copies, waits for them, and re-layouts  2.49 us (6%)
    pallas_call x1, Pallas kernels, shards(): pl.pallas_call(functools.partial(kernel, sizes), out_shape=jax.ShapeDtype...  40.9 us
    unnamed x5, local copies, waits for them, and re-layouts  2.49 us

profile of v2, /device:TPU:0, one launch (start us, length us, event | category | flops | bytes accessed | tf_op | source)
XLA Modules:
  0.0 43.4 jit_solution(2043068820968346226)
XLA Ops:
  0.0 0.0 copy-start
  0.0 0.9 %copy-done = f32[2,16,16,128]{3,2,1,0:T(8,128)S(1)} copy-done((f32[2,16,16,128]{3,2,1,0:T(8,128)S(1)}, f32[2,16,16,128]{3,2,1,0:T(8,128)}, u32[]{:S(2)}) %copy-start) | copy-done | bytes 262168
  1.0 0.0 copy-start.1
  1.0 0.8 %copy-done.1 = bf16[16,16,128]{2,1,0:T(8,128)(2,1)S(1)} copy-done((bf16[16,16,128]{2,1,0:T(8,128)(2,1)S(1)}, bf16[16,16,128]{2,1,0:T(8,128)(2,1)}, u32[]{:S(2)}) %copy-start.1) | copy-done | bytes 65560
  1.8 40.9 %shard_map.28 = f32[2,16,16,128]{3,2,1,0:T(8,128)S(1)} custom-call(f32[2,16,16,128]{3,2,1,0:T(8,128)S(1)} %copy-done, bf16[16,16,128]{2,1,0:T(8,128)(2,1)S(1)} %copy-done.1), custom_call_target="tpu_custom_call" | custom-call | tf_op jit(solution)/shard_map/pallas_call | solution.py:533
  42.7 0.7 %copy.4 = f32[2,16,16,128]{3,2,1,0:T(8,128)} copy(f32[2,16,16,128]{3,2,1,0:T(8,128)S(1)} %shard_map.28) | data formatting | bytes 524288
Async XLA Ops:
  0.0 0.9 %copy-start = (f32[2,16,16,128]{3,2,1,0:T(8,128)S(1)}, f32[2,16,16,128]{3,2,1,0:T(8,128)}, u32[]{:S(2)}) copy-start(f32[2,16,16,128]{3,2,1,0:T(8,128)} %g_hbm.1) | copy-start | bytes 786436
  1.0 0.8 %copy-start.1 = (bf16[16,16,128]{2,1,0:T(8,128)(2,1)S(1)}, bf16[16,16,128]{2,1,0:T(8,128)(2,1)}, u32[]{:S(2)}) copy-start(bf16[16,16,128]{2,1,0:T(8,128)(2,1)} %mach_hbm.1) | copy-start | bytes 196612

commit v3 on v2

--- a/solution.py
+++ b/solution.py
@@ -29,6 +29,10 @@
         if shift == 0:
             return value
     return pltpu.roll(value, shift, axis)
+
+
+def turn(shift):
+    return shift % LANES if isinstance(shift, int) else lax.rem(shift, LANES)
 
 
 def coefficients(mach, level):
@@ -48,7 +52,7 @@
     return value + jnp.where(even, roll(value, LANES - lanes, 1), roll(value, lanes, 1))
 
 
-def kernel(sizes, g_hbm, mach_hbm, out, g0, mach_in, in_sem, v0, v1, gl1, co0, co1, ys0, yr0, ys1, yr1, zs, zr, gm, gg,
+def kernel(sizes, g_hbm, mach_hbm, out, g0, mach_in, in_sem, tb, v0, v1, gl1, co0, co1, ys0, yr0, ys1, yr1, zs, zr, gm, gg,
            va, vb, vc, gc2, gc3, gc4, cc2, cc3, cc4, own, send_sem, recv_sem, gs_sem, gr_sem):
     nx, ny, nz = sizes
     count = nx * ny * nz
@@ -112,12 +116,13 @@
                 src_ref=src, dst_ref=dst, send_sem=send_sem.at[k, n], recv_sem=recv_sem.at[k, n],
                 device_id=to, device_id_type=MESH,
             )
-            pieces.append((copy, up if step > 0 else down, down if step > 0 else up))
+            pieces.append((copy, up if step > 0 else down, down if step > 0 else up, axis))
         return pieces
 
-    def start(L, r):
-        for copy, sends, _ in links(L, r):
-            pl.when(sends)(copy.start)
+    def start(L, r, axes=AXES):
+        for copy, sends, _, axis in links(L, r):
+            if axis in axes:
+                pl.when(sends)(copy.start)
 
     flying = []
 
@@ -125,11 +130,11 @@
         for earlier in flying:
             sent(*earlier)
         flying[:] = [(L, r)]
-        for copy, _, receives in links(L, r):
+        for copy, _, receives, _ in links(L, r):
             pl.when(receives)(copy.wait_recv)
 
     def sent(L, r):
-        for copy, sends, _ in links(L, r):
+        for copy, sends, _, _ in links(L, r):
             pl.when(sends)(copy.wait_send)
 
     def put(L, r, x, values, packed):
@@ -142,40 +147,67 @@
             packed = jnp.where(lane // 4 == x + 16 * c, roll(value, 4 * x + 2 + 64 * c, 1), packed)
         return packed
 
-    def seal(L, r, packed):
+    def seal(L, r, packed, axes=AXES):
         zs[4 * L["l"] + r] = packed
-        start(L, r)
+        start(L, r, axes)
 
     def sides(L, r):
         k, w = 4 * L["l"] + r, L["w"]
         below = (lane % 4 >= 2 - w) & (lane % 4 < 2)
         return jnp.where(below, zr[k, 0], roll(zr[k, 1], LANES - 2 * w, 1))
 
+    def inside(L, r):
+        v, w, co, g, X = L["v"], L["w"], L["co"], L["g"], L["X"]
+        scale = 0.25 ** L["l"]
+
+        def plane(x, west=True, east=True):
+            axial, drift = co[0, x], co[3, x]
+            t = []
+            for c in range(2):
+                value = v[r, c, x + 1]
+                lower = jnp.where(lane < w, 0.0, roll(value, w, 1))
+                upper = jnp.where(lane >= LANES - w, 0.0, roll(value, LANES - w, 1))
+                south = jnp.where(row < w, 0.0, roll(value, w, 0))
+                north = jnp.where(row >= Y0 - w, 0.0, roll(value, Y0 - w, 0))
+                t.append(g[c, x] + scale * ((lower + upper) + (south + north)))
+            e = [v[r, c, x + 2] for c in range(2)] if east else None
+            o = [v[r, c, x] for c in range(2)] if west else None
+            if east and west:
+                along = [e[c] + o[c] for c in range(2)]
+                slope = [e[c] - o[c] for c in range(2)]
+            elif east:
+                along, slope = e, e
+            else:
+                along, slope = o, [-o[0], -o[1]]
+            tb[0, x] = t[0] + axial * along[0] - drift * slope[1]
+            tb[1, x] = t[1] + axial * along[1] + drift * slope[0]
+
+        def middle(x, carry):
+            plane(x)
+            return carry
+
+        plane(0, west=False)
+        plane(X - 1, east=False)
+        lax.fori_loop(1, X - 1, middle, 0, unroll=True)
+
     def terms(L, r, x, side):
-        v, yr, w, co = L["v"], L["yr"], L["w"], L["co"]
+        v, yr, w, X, co = L["v"], L["yr"], L["w"], L["X"], L["co"]
         scale = 0.25 ** L["l"]
-        axial, drift = co[0, x], co[3, x]
-        centre, along, across = [], [], []
-        slope = []
-        for c in range(2):
-            here_ = v[r, c, x + 1]
-            east, west = v[r, c, x + 2], v[r, c, x]
-            shift = lax.rem(4 * LANES - (4 * x + 2 - w + 64 * c), LANES)
-            edge = roll(side, shift, 1)
-            lower = jnp.where(lane < w, edge, roll(here_, w, 1))
-            upper = jnp.where(lane >= LANES - w, edge, roll(here_, LANES - w, 1))
-            south = jnp.where(row < w, yr[r, 0, c, pl.ds(x, 1), :], roll(here_, w, 0))
-            north = jnp.where(row >= Y0 - w, yr[r, 1, c, pl.ds(x, 1), :], roll(here_, Y0 - w, 0))
-            centre.append(here_)
-            across.append((lower + upper) + (south + north))
-            along.append(east + west)
-            slope.append(east - west)
-        if L["l"]:
-            across = [scale * a for a in across]
-        g = L["g"]
-        real = g[0, x] + axial * along[0] + across[0] - drift * slope[1]
-        imaginary = g[1, x] + axial * along[1] + across[1] + drift * slope[0]
-        return centre, (real, imaginary)
+        rim = (lane < w) | (lane >= LANES - w)
+        t = []
+        for c in range(2):
+            shift = turn(4 * LANES - (4 * x + 2 - w + 64 * c))
+            add = jnp.where(rim, roll(side, shift, 1), 0.0)
+            south = jnp.where(row < w, yr[r, 0, c, pl.ds(x, 1), :], 0.0)
+            add = add + jnp.where(row >= Y0 - w, yr[r, 1, c, pl.ds(x, 1), :], south)
+            t.append(tb[c, x] + (scale * add if L["l"] else add))
+        if isinstance(x, int) and x in (0, X - 1):
+            axial, drift = co[0, x], co[3, x]
+            e = [v[r, c, 0 if x == 0 else X + 1] for c in range(2)]
+            if x == 0:
+                drift = -drift
+            t = [t[0] + axial * e[0] - drift * e[1], t[1] + axial * e[1] + drift * e[0]]
+        return [v[r, c, x + 1] for c in range(2)], t
 
     def relaxed(centre, t, hr, hi):
         return (0.5 * centre[0] + (hr * t[0] - hi * t[1]), 0.5 * centre[1] + (hi * t[0] + hr * t[1]))
@@ -186,27 +218,32 @@
         return (t[0] - dr * centre[0] + di * centre[1], t[1] - dr * centre[1] - di * centre[0])
 
     def relax(L, r):
+        inside(L, r)
         arrive(L, r)
         side = sides(L, r)
-        co = L["co"]
+        co, X = L["co"], L["X"]
 
         def body(x, packed):
             centre, t = terms(L, r, x, side)
             return put(L, r + 1, x, relaxed(centre, t, co[1, x], co[2, x]), packed)
 
-        seal(L, r + 1, lax.fori_loop(0, L["X"], body, jnp.zeros(tile, jnp.float32), unroll=True))
+        packed = body(X - 1, body(0, jnp.zeros(tile, jnp.float32)))
+        start(L, r + 1, "gx")
+        seal(L, r + 1, lax.fori_loop(1, X - 1, body, packed, unroll=True), ("gy", "gz"))
 
     def last(L, r, store):
+        inside(L, r)
         arrive(L, r)
         side = sides(L, r)
-        co = L["co"]
+        co, X = L["co"], L["X"]
 
         def body(x, carry):
             centre, t = terms(L, r, x, side)
             store(x, relaxed(centre, t, co[1, x], co[2, x]))
             return carry
 
-        lax.fori_loop(0, L["X"], body, 0, unroll=True)
+        body(X - 1, body(0, 0))
+        lax.fori_loop(1, X - 1, body, 0, unroll=True)
 
     def residual(L, r, x, side):
         centre, t = terms(L, r, x, side)
@@ -375,6 +412,7 @@
         over(D, body)
 
     relax(fine, 0)
+    inside(fine, 1)
     arrive(fine, 1)
     side = sides(fine, 1)
 
@@ -386,8 +424,10 @@
             gl1[c, x] = g[c]
         return put(half, 0, x, first(co1[1, x], co1[2, x], g[0], g[1]), packed)
 
-    packed = lax.fori_loop(0, X0 // 2, down_plane, jnp.zeros(tile, jnp.float32), unroll=True)
-    seal(half, 0, packed)
+    packed = down_plane(X0 // 2 - 1, down_plane(0, jnp.zeros(tile, jnp.float32)))
+    start(half, 0, "gx")
+    packed = lax.fori_loop(1, X0 // 2 - 1, down_plane, packed, unroll=True)
+    seal(half, 0, packed, ("gy", "gz"))
 
     bulk(gm, 0).wait_recv()
 
@@ -406,6 +446,7 @@
         over(D, body)
 
     relax(half, 0)
+    inside(half, 1)
     arrive(half, 1)
     side = sides(half, 1)
     groups = [jnp.zeros(tile, jnp.float32) for _ in range(2)]
@@ -506,6 +547,7 @@
             pltpu.VMEM(source.shape, f32),
             pltpu.VMEM(mach.shape, mach.dtype),
             pltpu.SemaphoreType.DMA((2,)),
+            pltpu.VMEM((2, X, Y, LANES), f32),
             pltpu.VMEM((4, 2, X + 2, Y, LANES), f32),
             pltpu.VMEM((4, 2, X // 2 + 2, Y, LANES), f32),
             pltpu.VMEM((2, X // 2, Y, LANES), f32),
@@ -533,7 +575,7 @@
         return pl.pallas_call(
             functools.partial(kernel, sizes),
             out_shape=jax.ShapeDtypeStruct(source.shape, f32),
-            in_specs=[pl.BlockSpec(memory_space=pl.ANY)] * 2,
+            in_specs=[pl.BlockSpec(memory_space=pltpu.HBM)] * 2,
             out_specs=pl.BlockSpec(memory_space=pltpu.VMEM),
             scratch_shapes=scratch,
             compiler_params=pltpu.CompilerParams(

time: 43.6 us -> 44.2 us (1.014)
  Pallas kernels: 40.9 us -> 41.5 us
    pallas_call x1, Pallas kernels: 40.9 us -> 41.5 us  [shards(): pl.pallas_call(functools.partial(kernel, sizes), out_shape=jax.ShapeDtype...]
where the time goes in v3:
time: 44.2 us; the launch traced here: 44 us
  Pallas kernels  41.5 us (94%)
  local copies, waits for them, and re-layouts  2.49 us (6%)
    pallas_call x1, Pallas kernels, shards(): pl.pallas_call(functools.partial(kernel, sizes), out_shape=jax.ShapeDtype...  41.5 us
    unnamed x5, local copies, waits for them, and re-layouts  2.49 us

profile of v3, /device:TPU:0, one launch (start us, length us, event | category | flops | bytes accessed | tf_op | source)
XLA Modules:
  0.0 44.0 jit_solution(8643554406228065832)
XLA Ops:
  0.0 0.0 copy-start
  0.0 0.9 %copy-done = f32[2,16,16,128]{3,2,1,0:T(8,128)S(1)} copy-done((f32[2,16,16,128]{3,2,1,0:T(8,128)S(1)}, f32[2,16,16,128]{3,2,1,0:T(8,128)}, u32[]{:S(2)}) %copy-start) | copy-done | bytes 262168
  1.0 0.0 copy-start.1
  1.0 0.8 %copy-done.1 = bf16[16,16,128]{2,1,0:T(8,128)(2,1)S(1)} copy-done((bf16[16,16,128]{2,1,0:T(8,128)(2,1)S(1)}, bf16[16,16,128]{2,1,0:T(8,128)(2,1)}, u32[]{:S(2)}) %copy-start.1) | copy-done | bytes 65560
  1.8 41.5 %shard_map.28 = f32[2,16,16,128]{3,2,1,0:T(8,128)S(1)} custom-call(f32[2,16,16,128]{3,2,1,0:T(8,128)S(1)} %copy-done, bf16[16,16,128]{2,1,0:T(8,128)(2,1)S(1)} %copy-done.1), custom_call_target="tpu_custom_call" | custom-call | tf_op jit(solution)/shard_map/pallas_call | solution.py:575
  43.3 0.7 %copy.4 = f32[2,16,16,128]{3,2,1,0:T(8,128)} copy(f32[2,16,16,128]{3,2,1,0:T(8,128)S(1)} %shard_map.28) | data formatting | bytes 524288
Async XLA Ops:
  0.0 0.9 %copy-start = (f32[2,16,16,128]{3,2,1,0:T(8,128)S(1)}, f32[2,16,16,128]{3,2,1,0:T(8,128)}, u32[]{:S(2)}) copy-start(f32[2,16,16,128]{3,2,1,0:T(8,128)} %g_hbm.1) | copy-start | bytes 786436
  1.0 0.8 %copy-start.1 = (bf16[16,16,128]{2,1,0:T(8,128)(2,1)S(1)}, bf16[16,16,128]{2,1,0:T(8,128)(2,1)}, u32[]{:S(2)}) copy-start(bf16[16,16,128]{2,1,0:T(8,128)(2,1)} %mach_hbm.1) | copy-start | bytes 196612

commit v4 on v2

--- a/solution.py
+++ b/solution.py
@@ -65,6 +65,22 @@
         t = lax.rem(me + d, count)
         return (t // (ny * nz), lax.rem(t // nz, ny), lax.rem(t, nz))
 
+    around = [[lax.rem(i + d, n) for d in range(n)] for i, n in zip((ix, iy, iz), sizes)]
+
+    def each_peer(act):
+        if count > 64:
+            def one(d, carry):
+                act(peer(d))
+                return carry
+
+            lax.fori_loop(1, count, one, 0)
+            return
+        for c in range(nz):
+            for a in range(nx):
+                for b in range(ny):
+                    if a or b or c:
+                        act((around[0][a], around[1][b], around[2][c]))
+
     loads = [
         pltpu.make_async_copy(mach_hbm, mach_in, in_sem.at[0]),
         pltpu.make_async_copy(g_hbm, g0, in_sem.at[1]),
@@ -73,9 +89,8 @@
         load.start()
     barrier = pltpu.get_barrier_semaphore()
 
-    def greet(d, carry):
-        pl.semaphore_signal(barrier, inc=1, device_id=peer(d), device_id_type=MESH)
-        return carry
+    def greet(to):
+        pl.semaphore_signal(barrier, inc=1, device_id=to, device_id_type=MESH)
 
     for ref in (v0, v1):
         zero = jnp.zeros((2,) + tile, jnp.float32)
@@ -85,7 +100,7 @@
     yr0[...] = jnp.zeros(yr0.shape, jnp.float32)
     yr1[...] = jnp.zeros(yr1.shape, jnp.float32)
     zr[...] = jnp.zeros(zr.shape, jnp.float32)
-    lax.fori_loop(1, count, greet, 0)
+    each_peer(greet)
 
     lane, row = lane_of(tile), row_of(tile)
     levels = (
@@ -253,20 +268,19 @@
         gm[me, y + 4:y + 5, :] = group[4 * y:4 * y + 1]
 
     def tell(ref, n):
-        def one(d, carry):
+        def one(to):
             pltpu.make_async_remote_copy(
                 src_ref=ref.at[me], dst_ref=ref.at[me], send_sem=gs_sem.at[n], recv_sem=gr_sem.at[n],
-                device_id=peer(d), device_id_type=MESH,
+                device_id=to, device_id_type=MESH,
             ).start()
-            return carry
-
-        lax.fori_loop(1, count, one, 0)
+
+        each_peer(one)
 
     def bulk(ref, n):
         part = ref.at[pl.ds(0, count - 1)]
         return pltpu.make_async_remote_copy(
             src_ref=part, dst_ref=part, send_sem=gs_sem.at[n], recv_sem=gr_sem.at[n],
-            device_id=peer(1), device_id_type=MESH,
+            device_id=(around[0][1], iy, iz), device_id_type=MESH,
         )
 
     def spread(ref, store):
@@ -533,11 +547,11 @@
         return pl.pallas_call(
             functools.partial(kernel, sizes),
             out_shape=jax.ShapeDtypeStruct(source.shape, f32),
-            in_specs=[pl.BlockSpec(memory_space=pl.ANY)] * 2,
+            in_specs=[pl.BlockSpec(memory_space=pltpu.HBM)] * 2,
             out_specs=pl.BlockSpec(memory_space=pltpu.VMEM),
             scratch_shapes=scratch,
             compiler_params=pltpu.CompilerParams(
-                collective_id=0, has_side_effects=True, vmem_limit_bytes=48 * 2**20
+                collective_id=0, has_side_effects=True, vmem_limit_bytes=60 * 2**20
             ),
         )(source, mach)
 

time: 43.6 us -> 42.9 us (0.984)
  local copies, waits for them, and re-layouts: 2.49 us -> 1.67 us
    unnamed x5 -> x1, local copies, waits for them, and re-layouts: 2.49 us -> 1.67 us
where the time goes in v4:
time: 42.9 us; the launch traced here: 42.5 us
  Pallas kernels  40.8 us (95%)
  local copies, waits for them, and re-layouts  1.67 us (4%)
    pallas_call x1, Pallas kernels, shards(): pl.pallas_call(functools.partial(kernel, sizes), out_shape=jax.ShapeDtype...  40.8 us
    unnamed x1, local copies, waits for them, and re-layouts  1.67 us

profile of v4, /device:TPU:0, one launch (start us, length us, event | category | flops | bytes accessed | tf_op | source)
XLA Modules:
  0.0 42.5 jit_solution(3196390756303576616)
XLA Ops:
  0.0 40.8 %shard_map.28 = f32[2,16,16,128]{3,2,1,0:T(8,128)} custom-call(f32[2,16,16,128]{3,2,1,0:T(8,128)} %g_hbm.1, bf16[16,16,128]{2,1,0:T(8,128)(2,1)} %mach_hbm.1), custom_call_target="tpu_custom_call" | custom-call | tf_op jit(solution)/shard_map/pallas_call | solution.py:547
  40.8 1.7 %copy.4 = f32[2,16,16,128]{3,2,1,0:T(8,128)} copy(f32[2,16,16,128]{3,2,1,0:T(8,128)} %shard_map.28) | data formatting | bytes 524288
